TPU v7x, 128 devices: a whole 4x4x4 slice. The times are simulated.
128 devices in a mesh: dp: 16 (over y_hi, x, core), tensor: 8 (over z, y_lo).
Axes of the slice: x: 4, y: 4 (y_hi: 2, y_lo: 2; y = y_hi * 2 + y_lo), z: 4, core: 2. Of those that a mesh axis runs over, the one named last changes fastest.
Arguments:
- learn_hidden: bfloat16 [768, 4096], P('dp', 'tensor'), may hold values from -360 to 360
- target_hidden: bfloat16 [768, 4096], P('dp', 'tensor'), may hold values from -360 to 360
- reward: bfloat16 [768], P('dp'), may hold values from -6 to 6
- learn_head: bfloat16 [4096, 128256], P(None, ('dp', 'tensor')), may hold values from -0.09375 to 0.09375
- target_head: bfloat16 [4096, 128256], P(None, ('dp', 'tensor')), may hold values from -0.09375 to 0.09375
- action: int32 [768], P('dp'), may hold values from 0 to 128255
- traj_len: int32 [32], P('dp'), may hold values from 1 to 24, 576 in all
- owner: int32 [32], P('dp'), may hold values from 0 to 15
Outputs:
- head_grad: bfloat16 [4096, 128256], P(None, ('dp', 'tensor'))
- hidden_grad: bfloat16 [768, 4096], P('dp', 'tensor')
- priority: float32 [16, 24], P('dp')
All inputs are finite; a program needn't handle non-finite values. No bound on the sum of `traj_len` on one device may be relied on, other than what follows from the above.
Results may differ from a plain program's by a relative error of at most 0.005.
Values may be sent and summed in bfloat16 or wider, within the bound.
No kernel may reach another device: no remote copies, remote signals or barrier semaphores. Data moves between devices by JAX's collectives and lax.ppermute only.
A program may use at most 128 MiB of HBM per device.

v0:
```python
import jax
import jax.numpy as jnp
from jax import lax
from jax.sharding import PartitionSpec as P

temper = 1.0
discount = 0.99
kl_weight = 10.0


def local_stats(logits):
    row_max = jnp.max(logits, axis=1)
    total = jnp.sum(jnp.exp((logits - row_max[:, None]) / temper), axis=1)
    return (row_max, total)


def shards(learn_hidden, target_hidden, reward, learn_head, target_head, action, traj_len, owner):
    learn_feat, target_feat = (
        lax.all_gather(learn_hidden, "tensor", axis=1, tiled=True),
        lax.all_gather(target_hidden, "tensor", axis=1, tiled=True),
    )
    learn_all, reward_all = (
        lax.all_gather(learn_feat, "dp", axis=0, tiled=True),
        lax.all_gather(reward, "dp", axis=0, tiled=True),
    )
    action_all, length_all, owner_all = (
        lax.all_gather(action, "dp", axis=0, tiled=True),
        lax.all_gather(traj_len, "dp", axis=0, tiled=True),
        lax.all_gather(owner, "dp", axis=0, tiled=True),
    )
    target_q = jnp.dot(
        lax.all_gather(target_feat, "dp", axis=0, tiled=True),
        target_head,
        preferred_element_type=jnp.float32,
    )
    learn_q = jnp.dot(learn_all, learn_head, preferred_element_type=jnp.float32)
    tokens = learn_all.shape[0]
    width = learn_head.shape[1]
    traj_count = length_all.shape[0]
    seq_len = tokens // traj_count
    block_index = lax.axis_index("dp") * lax.axis_size("tensor") + lax.axis_index("tensor")
    columns = block_index * width + jnp.arange(width, dtype=jnp.int32)
    hits = action_all[:, None] == columns[None, :]
    picked_part = jnp.sum(jnp.where(hits, learn_q, 0.0), axis=1)
    learn_peak, learn_part = local_stats(learn_q)
    target_peak, target_part = local_stats(target_q)
    learn_max, target_max = lax.pmax((learn_peak, target_peak), ("dp", "tensor"))
    learn_scaled = learn_part * jnp.exp((learn_peak - learn_max) / temper)
    target_scaled = target_part * jnp.exp((target_peak - target_max) / temper)
    learn_sum, target_sum, picked = lax.psum(
        (learn_scaled, target_scaled, picked_part), ("dp", "tensor")
    )
    target_value = target_max + temper * jnp.log(target_sum)
    learn_p = jnp.exp((learn_q - learn_max[:, None]) / temper) / learn_sum[:, None]
    target_p = jnp.exp((target_q - target_max[:, None]) / temper) / target_sum[:, None]
    position = jnp.arange(tokens, dtype=jnp.int32)
    offset = position % seq_len
    lengths = jnp.repeat(length_all, seq_len)
    live = (offset < lengths).astype(jnp.float32)
    follow = (offset + 1 < lengths).astype(jnp.float32)
    shifted = jnp.concatenate([target_value[1:], jnp.zeros((1,), jnp.float32)])
    target_y = reward_all.astype(jnp.float32) + discount * follow * shifted
    delta = live * (picked - target_y)
    grad_q = (
        jnp.where(hits, delta[:, None], 0.0)
        + kl_weight * live[:, None] * (learn_p - target_p) / temper
    ) / traj_count
    grad_q = grad_q.astype(jnp.bfloat16)
    head_grad = lax.dot_general(
        learn_all, grad_q, (((0,), (0,)), ((), ())), preferred_element_type=jnp.float32
    ).astype(jnp.bfloat16)
    row_sums = lax.psum_scatter(
        lax.dot_general(
            grad_q, learn_head, (((1,), (1,)), ((), ())), preferred_element_type=jnp.float32
        ),
        "dp",
        scatter_dimension=0,
        tiled=True,
    )
    hidden_grad = lax.psum_scatter(row_sums, "tensor", scatter_dimension=1, tiled=True)
    hidden_grad = hidden_grad.astype(jnp.bfloat16)
    owners_all = lax.axis_size("dp")
    magnitude = jnp.abs(delta).reshape(traj_count, seq_len)
    owner_table = (jnp.arange(owners_all, dtype=jnp.int32)[:, None] == owner_all[None, :]).astype(
        jnp.float32
    )
    sums = jnp.dot(owner_table, magnitude, precision=lax.Precision.HIGHEST)
    priority = lax.dynamic_slice_in_dim(sums, lax.axis_index("dp"), 1, 0)
    return (head_grad, hidden_grad, priority)


def solution(mesh):
    return jax.shard_map(
        shards,
        mesh=mesh,
        in_specs=(
            P("dp", "tensor"),
            P("dp", "tensor"),
            P("dp"),
            P(None, ("dp", "tensor")),
            P(None, ("dp", "tensor")),
            P("dp"),
            P("dp"),
            P("dp"),
        ),
        out_specs=(P(None, ("dp", "tensor")), P("dp", "tensor"), P("dp", None)),
        check_vma=False,
    )
```

profile of v0, /device:TPU:0, one launch (start us, length us, event | category | flops | bytes accessed | tf_op | source)
XLA Modules:
  0.0 498.0 jit_solution(7546959880714166229)
XLA Ops:
  7.2 0.0 all-gather.3.cloned.1.call-start
  7.2 32.9 %all_gather.26 = bf16[48,4096]{1,0:T(8,128)(2,1)} all-gather(bf16[48,512]{1,0:T(8,128)(2,1)} %param.8), channel_id=1, replica_groups=mesh['dp'=16,'tensor'=8] {'tensor'}, dimensions={1}, use_global_device_ids=true | all-gather | bytes 442368 | tf_op jit(solution)/shard_map/all_gather | solution.py:19
  40.1 0.0 all-gather.3.cloned.1.call-update
  40.2 0.0 all-gather.5.cloned.1.call-start
  40.2 32.3 %all_gather.29 = bf16[48,4096]{1,0:T(8,128)(2,1)} all-gather(bf16[48,512]{1,0:T(8,128)(2,1)} %param.9), channel_id=1, replica_groups=mesh['dp'=16,'tensor'=8] {'tensor'}, dimensions={1}, use_global_device_ids=true | all-gather | bytes 442368 | tf_op jit(solution)/shard_map/all_gather | solution.py:20
  72.6 0.0 all-gather.5.cloned.1.call-update
  72.6 0.0 reduce-scatter.3.cloned.1.call-start
  72.6 1.2 dynamic-slice
  75.2 0.9 dynamic-update-slice.1
  76.1 0.8 dynamic-update-slice.3
  76.9 0.8 dynamic-update-slice
  77.8 14.5 %all-reduce.4 = (s32[768]{0:T(1024)S(1)}, s32[32]{0:T(128)S(1)}, s32[32]{0:T(128)S(1)}) all-reduce(s32[768]{0:T(1024)S(1)} %dynamic-update-slice, s32[32]{0:T(128)S(1)} %dynamic-update-slice.1, s32[32]{0:T(128)S(1)} %dynamic-update-slice.3), channel_id=1, replica_groups=mesh['dp'=16,'tensor'=8] {'dp'}, use_global_device_ids=true, to_apply=%add | all-reduce | flops 832 | bytes 6656
  92.2 0.1 broadcast_in_dim.12
  92.3 0.1 reshape.41
  92.4 0.8 dynamic-update-slice.2
  93.2 33.4 %all-reduce.2 = bf16[768]{0:T(1024)(128)(2,1)S(1)} all-reduce(bf16[768]{0:T(1024)(128)(2,1)S(1)} %dynamic-update-slice.2), channel_id=1, replica_groups=mesh['dp'=16,'tensor'=8] {'dp'}, use_global_device_ids=true, to_apply=%add.2 | all-reduce | flops 768 | bytes 3072
  126.7 0.0 all-gather.3.cloned.1.call-done
  126.7 10.9 %fusion.19 = (f32[768]{0:T(1024)S(1)}, f32[768,1002]{0,1:T(8,128)S(1)}) fusion(bf16[768,4096]{1,0:T(8,128)(2,1)} %all-gather.3.cloned.1.call-done, bf16[4096,1002]{0,1:T(8,128)(2,1)} %param.11), kind=kOutput, calls=%fused_computation.32 | convolution fusion | flops 6304807936 | bytes 17581056 | tf_op jit(solution)/shard_map/dot_general | solution.py:36
  137.6 34.3 %all-gather.5.cloned.1.call-done = bf16[768,4096]{1,0:T(8,128)(2,1)} async-done(((bf16[48,4096]{1,0:T(8,128)(2,1)}), bf16[768,4096]{1,0:T(8,128)(2,1)}) %all-gather.5.cloned.1.call-update) | async-done | bytes 6291472 | tf_op jit(solution)/shard_map/all_gather | solution.py:32
  172.0 12.1 %fusion.18 = (f32[768]{0:T(1024)S(1)}, f32[768,1002]{0,1:T(8,128)}) fusion(bf16[768,4096]{1,0:T(8,128)(2,1)} %all-gather.5.cloned.1.call-done, bf16[4096,1002]{0,1:T(8,128)(2,1)} %param.12), kind=kOutput, calls=%fused_computation.31 | convolution fusion | flops 6304807936 | bytes 17581056 | tf_op jit(solution)/shard_map/dot_general | solution.py:31
  184.0 64.8 %all-reduce.6 = (f32[768]{0:T(1024)S(1)}, f32[768]{0:T(1024)S(1)}) all-reduce(f32[768]{0:T(1024)S(1)} %get-tuple-element.16, f32[768]{0:T(1024)S(1)} %get-tuple-element.18), channel_id=1, replica_groups=mesh['dp'=16,'tensor'=8] {'dp','tensor'}, use_global_device_ids=true, to_apply=%region_3.4 | all-reduce | flops 1536 | bytes 12288 | tf_op jit(solution)/shard_map/pmax | solution.py:47
  248.8 2.4 exponential_reduce_fusion.1
  251.2 0.7 fusion
  251.9 64.3 %all-reduce.5 = (f32[768]{0:T(1024)S(1)}, f32[768]{0:T(1024)S(1)}, f32[768]{0:T(1024)S(1)}) all-reduce(f32[768]{0:T(1024)S(1)} %get-tuple-element.21, f32[768]{0:T(1024)S(1)} %get-tuple-element.20, f32[768]{0:T(1024)S(1)} %get-tuple-element.3), channel_id=1, replica_groups=mesh['dp'=16,'tensor'=8] {'dp','tensor'}, use_global_device_ids=true, to_apply=%region_5.6 | all-reduce | flops 2304 | bytes 18432 | tf_op jit(solution)/shard_map/psum | solution.py:50
  316.2 0.1 slice.3
  316.3 0.1 fusion.16
  316.4 14.2 %fusion.13 = f32[768,4096]{1,0:T(8,128)} fusion(bf16[4096,1002]{0,1:T(8,128)(2,1)} %param.11, f32[768,1002]{0,1:T(8,128)} %get-tuple-element.17, f32[768,1002]{0,1:T(8,128)S(1)} %get-tuple-element.19, f32[768]{0:T(1024)S(1)} %get-tuple-element.8, f32[768]{0:T(1024)S(1)} %get-tuple-element.11, f32[768]{0:T(1024)S(1)} %get-tuple-element.9, ...), kind=kOutput, calls=%fused_computation.29 | convolution fusion | flops 6312503808 | bytes 26973096 | tf_op jit(solution)/shard_map/dot_general | solution.py:73
  330.6 0.0 reduce-scatter.3.cloned.1.call-update
  330.7 0.0 reduce-scatter.5.cloned.1.call-start
  330.7 0.1 reshape.42
  330.8 0.1 fusion.4
  330.9 0.5 constant_dynamic-slice_fusion
  331.4 117.7 %reduce-scatter.3.cloned.1.call-done = f32[48,4096]{1,0:T(8,128)} async-done(((f32[768,4096]{1,0:T(8,128)}), f32[48,4096]{1,0:T(8,128)}) %reduce-scatter.3.cloned.1.call-update) | async-done | bytes 786448 | tf_op jit(solution)/shard_map/reduce_scatter | solution.py:72
  449.2 0.0 reduce-scatter.5.cloned.1.call-update
  449.2 13.4 %convert_bitcast_fusion = bf16[4096,1002]{0,1:T(8,128)(2,1)} fusion(bf16[768,4096]{1,0:T(8,128)(2,1)} %all-gather.3.cloned.1.call-done, f32[768,1002]{0,1:T(8,128)} %get-tuple-element.17, f32[768,1002]{0,1:T(8,128)S(1)} %get-tuple-element.19, f32[768]{0:T(1024)S(1)} %get-tuple-element.8, f32[768]{0:T(1024)S(1)} %get-tuple-element.11, ...), kind=kOutput, calls=%fused_computation | convolution fusion | flops 6316608000 | bytes 20681640 | tf_op jit(solution)/shard_map/dot_general | solution.py:69
  462.6 27.4 %reduce-scatter.5.cloned.1.call-done = f32[48,512]{1,0:T(8,128)} async-done(((f32[48,4096]{1,0:T(8,128)}), f32[48,512]{1,0:T(8,128)}) %reduce-scatter.5.cloned.1.call-update) | async-done | bytes 98320 | tf_op jit(solution)/shard_map/reduce_scatter | solution.py:80
  490.0 1.5 convert_element_type.23
  (7 shorter events, 0.0 us)
Async XLA Ops:
  7.2 119.5 %all-gather.3.cloned.1.call-start = ((), (), s32[]{:S(2)}) async-start(), calls=%async_computation.2 | async-start | bytes 6684672 | tf_op jit(solution)/shard_map/all_gather | solution.py:23
  40.2 131.8 %all-gather.5.cloned.1.call-start = ((), (), s32[]{:S(2)}) async-start(), calls=%async_computation.3 | async-start | bytes 6684672 | tf_op jit(solution)/shard_map/all_gather | solution.py:32
  72.6 376.6 %reduce-scatter.3.cloned.1.call-start = ((), (), s32[]{:S(2)}) async-start(), calls=%async_computation.4 | async-start | bytes 13369344 | tf_op jit(solution)/shard_map/reduce_scatter | solution.py:72
  330.7 159.3 %reduce-scatter.5.cloned.1.call-start = ((), (), s32[]{:S(2)}) async-start(), calls=%async_computation.5 | async-start | bytes 884736 | tf_op jit(solution)/shard_map/reduce_scatter | solution.py:80
Sparse Core Ops, SparseCore 0:
  40.3 66.5 all-gather.2
  109.4 62.5 all-gather.4
  330.8 118.3 reduce-scatter.2
  451.5 38.3 reduce-scatter.4
where the time goes:
time: 499 us; the launch traced here: 498 us
  blocking collectives  242 us (48%)
  waiting for transfers between devices  180 us (36%)
  matrix products  50.7 us (10%)
  between operations  15.1 us (3%)
  local copies, waits for them, and re-layouts  5.49 us (1%)
    reduce_scatter x1, waiting for transfers between devices, shards(): lax.psum_scatter(lax.dot_general(grad_q, learn_head, (((1,), (1,)), ((),...  118 us
    pmax x1, blocking collectives, shards(): lax.pmax((learn_peak, target_peak), ('dp', 'tensor'))  64.8 us
    psum x1, blocking collectives, shards(): lax.psum((learn_scaled, target_scaled, picked_part), ('dp', 'tensor'))  64.3 us
    unnamed x2, blocking collectives  47.9 us
    all_gather x1, waiting for transfers between devices, shards(): lax.all_gather(target_feat, 'dp', axis=0, tiled=True)  34.3 us
    all_gather x1, blocking collectives, shards(): lax.all_gather(learn_hidden, 'tensor', axis=1, tiled=True)  32.9 us
    all_gather x1, blocking collectives, shards(): lax.all_gather(target_hidden, 'tensor', axis=1, tiled=True)  32.3 us
    reduce_scatter x1, waiting for transfers between devices, shards(): lax.psum_scatter(row_sums, 'tensor', scatter_dimension=1, tiled=True)  27.4 us
  transfers between devices with their start and end apart: 4, of which 3 were waited for; matrix products, arithmetic and copies ran while one was open for 6% of the time, Pallas kernels for 0%

commit v1 on v0

v1 whole, which is shorter than its diff:
```python
import functools

import jax
import jax.numpy as jnp
from jax import lax
from jax.experimental import pallas as pl
from jax.experimental.pallas import tpu as pltpu
from jax.sharding import Mesh, PartitionSpec as P

temper = 1.0
discount = 0.99
kl_weight = 10.0

DP = ("yh", "x", "c")
TENSOR = ("z", "yl")
PLANE = ("yh", "x", "z", "yl")
Y = ("yh", "yl")


def shift(v, axis, by):
    return lax.ppermute(v, axis, [(i, (i + by) % 4) for i in range(4)])


def swap_cores(v):
    return lax.ppermute(v, "c", [(0, 1), (1, 0)])


def gather_ring(v, axis):
    me = lax.axis_index(axis)
    arrived = [v] + [shift(v, axis, by) for by in (1, 3, 2)]
    out = jnp.zeros((4,) + v.shape, v.dtype)
    for by, block in zip((0, 1, 3, 2), arrived):
        out = lax.dynamic_update_index_in_dim(out, block, (me - by) & 3, 0)
    return out


VMEM_LIMIT = 40 * 1024 * 1024
NT = (((1,), (1,)), ((), ()))
NN = (((1,), (0,)), ((), ()))


def whole(shape):
    return pl.BlockSpec(shape, lambda j: (0,) * len(shape))


def hidden_spec(shape, x_first):
    rows, feats = shape[-2:]
    if x_first:
        return pl.BlockSpec((4, 2, 1, 1, rows, feats), lambda j: (0, 0, j % 2, j // 2, 0, 0))
    return pl.BlockSpec((2, 1, 4, 1, rows, feats), lambda j: (0, j % 2, 0, j // 2, 0, 0))


def hidden_block(ref, x_first):
    rows, feats = ref.shape[-2:]
    if x_first:
        return jnp.concatenate([ref[x, yh, 0, 0] for yh in range(2) for x in range(4)], axis=0)
    return ref[...].reshape(8 * rows, feats)


def cost(flops, nbytes, exps=0):
    return pl.CostEstimate(flops=flops, bytes_accessed=nbytes, transcendentals=exps)


def q_kernel(x_first, row, base_ref, action_ref, hidden_ref, own_ref, sib_ref, q_own, q_sib, stats_ref):
    j = pl.program_id(0)
    hidden = hidden_block(hidden_ref, x_first)
    for head_ref, q_ref in ((own_ref, q_own), (sib_ref, q_sib)):
        part = lax.dot_general(head_ref[...], hidden, NT, preferred_element_type=jnp.float32)

        @pl.when(j == 0)
        def _():
            q_ref[...] = part

        @pl.when(j > 0)
        def _():
            q_ref[...] += part

    @pl.when(j == pl.num_programs(0) - 1)
    def _():
        peak = jnp.maximum(
            jnp.max(q_own[...], axis=0, keepdims=True), jnp.max(q_sib[...], axis=0, keepdims=True)
        )
        total = jnp.zeros_like(peak)
        picked = jnp.zeros_like(peak)
        ids = lax.broadcasted_iota(jnp.int32, q_own.shape, 0)
        for k, q_ref in enumerate((q_own, q_sib)):
            q = q_ref[...]
            total += jnp.sum(jnp.exp((q - peak) / temper), axis=0, keepdims=True)
            if row == 0:
                hit = ids == action_ref[...] - base_ref[k]
                picked += jnp.sum(jnp.where(hit, q, 0.0), axis=0, keepdims=True)
        stats_ref[...] = jnp.zeros_like(stats_ref)
        stats_ref[row : row + 1] = peak
        stats_ref[row + 1 : row + 2] = total
        if row == 0:
            stats_ref[4:5] = picked


def q_values(hidden, heads, bases, action, x_first, row):
    width, feats_all = heads[0].shape
    feats = hidden.shape[-1]
    tokens = action.shape[1]
    steps = feats_all // feats
    head_spec = pl.BlockSpec((width, feats), lambda j: (0, j))
    q_shape = jax.ShapeDtypeStruct((width, tokens), jnp.float32)
    return pl.pallas_call(
        functools.partial(q_kernel, x_first, row),
        grid=(steps,),
        in_specs=[
            pl.BlockSpec(memory_space=pltpu.SMEM),
            whole(action.shape),
            hidden_spec(hidden.shape, x_first),
            head_spec,
            head_spec,
        ],
        out_specs=[whole(q_shape.shape)] * 2 + [whole((8, tokens))],
        out_shape=[q_shape, q_shape, jax.ShapeDtypeStruct((8, tokens), jnp.float32)],
        compiler_params=pltpu.CompilerParams(vmem_limit_bytes=VMEM_LIMIT),
        cost_estimate=cost(
            4 * tokens * width * feats_all, 4 * width * feats_all + 2 * tokens * feats_all, 2 * tokens * width
        ),
    )(bases, action, hidden, *heads)


def grad_kernel(
    scale, base_ref, action_ref, vec_ref, lq_own, lq_sib, tq_own, tq_sib, own_ref, sib_ref,
    grad_own, grad_sib, part_ref, g_own, g_sib,
):
    @pl.when(pl.program_id(0) == 0)
    def _():
        learn_max, learn_gain, target_max, target_gain, delta = (vec_ref[k : k + 1] for k in range(5))
        ids = lax.broadcasted_iota(jnp.int32, lq_own.shape, 0)
        for k, (lq, tq, out, flat) in enumerate(
            ((lq_own, tq_own, grad_own, g_own), (lq_sib, tq_sib, grad_sib, g_sib))
        ):
            learn_p = jnp.exp((lq[...] - learn_max) / temper) * learn_gain
            target_p = jnp.exp((tq[...] - target_max) / temper) * target_gain
            hit = ids == action_ref[...] - base_ref[k]
            grad = (jnp.where(hit, delta, 0.0) + (learn_p - target_p) / temper) * scale
            out[...] = grad.astype(jnp.bfloat16)
            flat[...] = grad.T.astype(jnp.bfloat16)

    part = lax.dot_general(g_own[...], own_ref[...], NN, preferred_element_type=jnp.float32)
    part += lax.dot_general(g_sib[...], sib_ref[...], NN, preferred_element_type=jnp.float32)
    part_ref[...] = part.astype(jnp.bfloat16).reshape(part_ref.shape)


def gradients(lq, tq, heads, bases, action, vec, rows, feats, traj_total):
    width, feats_all = heads[0].shape
    tokens = action.shape[1]
    steps = feats_all // feats
    head_spec = pl.BlockSpec((width, feats), lambda j: (0, j))
    g_shape = jax.ShapeDtypeStruct((width, tokens), jnp.bfloat16)
    return pl.pallas_call(
        functools.partial(grad_kernel, 1.0 / traj_total),
        grid=(steps,),
        in_specs=[pl.BlockSpec(memory_space=pltpu.SMEM), whole(action.shape), whole(vec.shape)]
        + [whole((width, tokens))] * 4
        + [head_spec] * 2,
        out_specs=[whole((width, tokens))] * 2
        + [pl.BlockSpec((tokens // rows, 1, rows, feats), lambda j: (0, j, 0, 0))],
        out_shape=[g_shape, g_shape]
        + [jax.ShapeDtypeStruct((tokens // rows, steps, rows, feats), jnp.bfloat16)],
        scratch_shapes=[pltpu.VMEM((tokens, width), jnp.bfloat16)] * 2,
        compiler_params=pltpu.CompilerParams(vmem_limit_bytes=VMEM_LIMIT),
        cost_estimate=cost(
            4 * tokens * width * feats_all, 4 * width * feats_all + 2 * tokens * feats_all, 4 * tokens * width
        ),
    )(bases, action, vec, *lq, *tq, *heads)


def head_kernel(x_first, grad_ref, hidden_ref, *refs):
    out_ref = refs[-1]
    total = lax.dot_general(
        grad_ref[...], hidden_block(hidden_ref, x_first), NN, preferred_element_type=jnp.float32
    )
    if len(refs) > 1:
        total += refs[0][...].astype(jnp.float32)
    out_ref[...] = total.astype(jnp.bfloat16)


def head_part(grad, hidden, x_first, *more):
    width, tokens = grad.shape
    feats = hidden.shape[-1]
    steps = 8
    spec = pl.BlockSpec((width, feats), lambda j: (0, j))
    return pl.pallas_call(
        functools.partial(head_kernel, x_first),
        grid=(steps,),
        in_specs=[whole(grad.shape), hidden_spec(hidden.shape, x_first)] + [spec] * len(more),
        out_specs=spec,
        out_shape=jax.ShapeDtypeStruct((width, steps * feats), jnp.bfloat16),
        compiler_params=pltpu.CompilerParams(vmem_limit_bytes=VMEM_LIMIT),
        cost_estimate=cost(
            2 * tokens * width * steps * feats, (2 * width + 2 * tokens + 2 * width * len(more)) * steps * feats
        ),
    )(grad, hidden, *more)


def shards(learn_hidden, target_hidden, reward, learn_head, target_head, action, traj_len, owner):
    f32, bf16 = jnp.float32, jnp.bfloat16
    rows, feats = learn_hidden.shape
    width = learn_head.shape[1]
    trajs = traj_len.shape[0]
    tokens = rows * 8
    seq_len = rows // trajs
    traj_total = trajs * 16

    learn_head, target_head = learn_head.T, target_head.T
    learn_sib, target_sib = swap_cores(learn_head), swap_cores(target_head)

    small = jnp.concatenate(
        [action.astype(f32), reward.astype(f32), traj_len.astype(f32), owner.astype(f32)]
    )
    small = jnp.pad(small, (0, 128 - small.shape[0]))

    both = gather_ring(jnp.stack([learn_hidden, target_hidden]), "z")
    learn = gather_ring(both[:, 0], "x")
    target = gather_ring(both[:, 1], Y)
    learn, target, learn_sib, target_sib, small = lax.optimization_barrier(
        (learn, target, learn_sib, target_sib, small)
    )
    learn = gather_ring(learn, Y).reshape(2, 2, 4, 4, rows, feats)
    target = gather_ring(target, "x").reshape(4, 2, 2, 4, rows, feats)
    learn_heads, target_heads = (learn_head, learn_sib), (target_head, target_sib)

    small = lax.all_to_all(
        jnp.broadcast_to(small[None, None], (8, 8, 128)), ("yh", "x"), 0, 0, tiled=True
    )[:, 0]
    action_all = small[:, :rows].reshape(1, tokens).astype(jnp.int32)
    reward_all = small[:, rows : 2 * rows].reshape(tokens)
    length_all = small[:, 2 * rows : 2 * rows + trajs].reshape(8 * trajs).astype(jnp.int32)
    owner_all = small[:, 2 * rows + trajs : 2 * rows + 2 * trajs].reshape(8 * trajs).astype(jnp.int32)

    core = lax.axis_index("c")
    dp = lax.axis_index(DP)
    tensor = lax.axis_index(TENSOR)
    bases = jnp.stack([((dp + (1 - 2 * core) * k) * 8 + tensor) * width for k in (0, 1)])

    *learn_q, learn_stats = q_values(learn, learn_heads, bases, action_all, False, 0)
    *target_q, target_stats = q_values(target, target_heads, bases, action_all, True, 2)

    packed = learn_stats + target_stats
    packed = lax.all_to_all(
        jnp.broadcast_to(packed[None], (64,) + packed.shape), PLANE, 0, 0, tiled=True
    )
    learn_max = jnp.max(packed[:, 0], axis=0)
    target_max = jnp.max(packed[:, 2], axis=0)
    learn_sum = jnp.sum(packed[:, 1] * jnp.exp((packed[:, 0] - learn_max) / temper), axis=0)
    target_sum = jnp.sum(packed[:, 3] * jnp.exp((packed[:, 2] - target_max) / temper), axis=0)
    picked = jnp.sum(packed[:, 4], axis=0)

    target_value = target_max + temper * jnp.log(target_sum)
    offset = jnp.arange(tokens, dtype=jnp.int32) % seq_len
    lengths = jnp.repeat(length_all, seq_len)
    live = (offset < lengths).astype(f32)
    follow = (offset + 1 < lengths).astype(f32)
    shifted = jnp.concatenate([target_value[1:], jnp.zeros((1,), f32)])
    target_y = reward_all + discount * follow * shifted
    delta = live * (picked - target_y)

    zero = jnp.zeros_like(delta)
    vec = jnp.stack(
        [
            learn_max,
            kl_weight * live / learn_sum,
            target_max,
            kl_weight * live / target_sum,
            delta,
            zero,
            zero,
            zero,
        ]
    )
    grad_own, grad_sib, partial = gradients(
        learn_q, target_q, learn_heads, bases, action_all, vec, rows, feats, traj_total
    )

    partial = lax.all_to_all(partial.reshape(64, rows, feats), PLANE, 0, 0, tiled=True)
    hidden_grad = jnp.sum(partial.astype(f32), axis=0).astype(bf16)

    theirs = swap_cores(head_part(grad_sib, learn, False))
    head_grad = head_part(grad_own, learn, False, theirs).T

    magnitude = jnp.abs(delta).reshape(8 * trajs, seq_len)
    owner_table = (jnp.arange(16, dtype=jnp.int32)[:, None] == owner_all[None, :]).astype(f32)
    sums = jnp.dot(owner_table, magnitude, precision=lax.Precision.HIGHEST)
    sums = sums + swap_cores(sums)
    priority = lax.dynamic_slice_in_dim(sums, dp, 1, 0)
    return (head_grad, hidden_grad, priority)


def solution(mesh):
    fine = Mesh(mesh.devices.reshape(2, 4, 2, 4, 2), ("yh", "x", "c", "z", "yl"))
    vocab = P(None, DP + TENSOR)
    return jax.shard_map(
        shards,
        mesh=fine,
        in_specs=(P(DP, TENSOR), P(DP, TENSOR), P(DP), vocab, vocab, P(DP), P(DP), P(DP)),
        out_specs=(vocab, P(DP, TENSOR), P(DP, None)),
        check_vma=False,
    )
```

time: 499 us -> 244 us (0.49)
  blocking collectives: 242 us -> 0 us
  waiting for transfers between devices: 180 us -> 73.2 us
  Pallas kernels: 0 us -> 66.7 us
  matrix products: 50.7 us -> 0.19 us
  starting transfers between devices: 0.16 us -> 47.6 us
  local copies, waits for them, and re-layouts: 5.49 us -> 42.9 us
  between operations: 15.1 us -> 0.93 us
  other arithmetic: 4.71 us -> 11.4 us
    reduce_scatter x2 -> x0, waiting for transfers between devices: 145 us -> none  [the longest x1 118 us: shards(): lax.psum_scatter(lax.dot_general(grad_q, learn_head, (((1,), (1,)), ((),...]
    pallas_call x0 -> x5, Pallas kernels: none -> 66.7 us  [the longest x2 35.1 us: q_values(): pl.pallas_call(functools.partial(q_kernel, x_first, row), grid=(steps,),...]
    all_gather x2 -> x0, blocking collectives: 65.3 us -> none  [the longest x1 32.9 us: shards(): lax.all_gather(learn_hidden, 'tensor', axis=1, tiled=True)]
    pmax x1 -> x0, blocking collectives: 64.8 us -> none  [shards(): lax.pmax((learn_peak, target_peak), ('dp', 'tensor'))]
    psum x1 -> x0, blocking collectives: 64.3 us -> none  [shards(): lax.psum((learn_scaled, target_scaled, picked_part), ('dp', 'tensor'))]
    all_to_all x0 -> x3, waiting for transfers between devices: none -> 62.5 us  [the longest x1 34.6 us: shards(): lax.all_to_all(partial.reshape(64, rows, feats), PLANE, 0, 0, tiled=True)]
    dot_general x4 -> x0, matrix products: 50.6 us -> none  [the longest x1 14.2 us: shards(): lax.dot_general(grad_q, learn_head, (((1,), (1,)), ((), ())), preferred_e...]
    unnamed x2 -> x0, blocking collectives: 47.9 us -> none
  transfers between devices with their start and end apart: 4 -> 22, of which waited for: 3 -> 8; matrix products, arithmetic and copies ran while one was open for 6% -> 13% of each run, Pallas kernels for 0% -> 7%
where the time goes in v1:
time: 244 us; the launch traced here: 243 us
  waiting for transfers between devices  73.2 us (30%)
  Pallas kernels  66.7 us (27%)
  starting transfers between devices  47.6 us (20%)
  local copies, waits for them, and re-layouts  42.9 us (18%)
  other arithmetic  11.4 us (5%)
    pallas_call x2, Pallas kernels, q_values(): pl.pallas_call(functools.partial(q_kernel, x_first, row), grid=(steps,),...  35.1 us
    all_to_all x1, waiting for transfers between devices, shards(): lax.all_to_all(partial.reshape(64, rows, feats), PLANE, 0, 0, tiled=True)  34.6 us
    ppermute x15, starting transfers between devices, shift(): return lax.ppermute(v, axis, [(i, (i + by) % 4) for i in range(4)])  28.7 us
    unnamed x26, local copies, waits for them, and re-layouts  18.5 us
    pallas_call x2, Pallas kernels, head_part(): pl.pallas_call(functools.partial(head_kernel, x_first), grid=(steps,), in...  18.3 us
    dynamic_update_slice x19, local copies, waits for them, and re-layouts, gather_ring(): out = lax.dynamic_update_index_in_dim(out, block, me - by & 3, 0)  17.6 us
    all_to_all x1, waiting for transfers between devices, shards(): lax.all_to_all(jnp.broadcast_to(small[None, None], (8, 8, 128)), ('yh', '...  16.2 us
    pallas_call x1, Pallas kernels, gradients(): pl.pallas_call(functools.partial(grad_kernel, 1.0 / traj_total), grid=(st...  13.3 us
  transfers between devices with their start and end apart: 22, of which 8 were waited for; matrix products, arithmetic and copies ran while one was open for 13% of the time, Pallas kernels for 7%

profile of v1, /device:TPU:0, one launch (start us, length us, event | category | flops | bytes accessed | tf_op | source)
XLA Modules:
  0.0 242.9 jit_solution(4963586187287921238)
XLA Ops:
  2.1 2.1 collective-permute-start
  4.1 2.2 collective-permute-start.1
  6.3 1.8 collective-permute-start.2
  12.6 1.6 collective-permute-start.6
  14.3 1.7 collective-permute-start.7
  15.9 2.0 collective-permute-start.8
  17.9 1.0 broadcast.145.clone.1
  21.3 1.5 collective-permute-start.3
  23.5 2.8 %collective-permute-start.4 = (bf16[4,48,512]{2,1,0:T(8,128)(2,1)S(1)}, bf16[4,48,512]{2,1,0:T(8,128)(2,1)S(1)}, u32[]{:S(2)}, u32[]{:S(2)}) collective-permute-start(bf16[4,48,512]{2,1,0:T(8,128)(2,1)S(1)} %get-tuple-element.42), channel_id=1, source_target_pairs={{0,48},{16,0},{32,16},{48,32},{1,49},{17,1},{33,17},{49,33},{2,50}... | collective-permute-start | bytes 589832 | tf_op jit(solution)/shard_map/ppermute | solution.py:21
  27.0 1.4 collective-permute-start.5
  29.8 3.6 %collective-permute-done.4 = bf16[4,48,512]{2,1,0:T(8,128)(2,1)S(1)} collective-permute-done((bf16[4,48,512]{2,1,0:T(8,128)(2,1)S(1)}, bf16[4,48,512]{2,1,0:T(8,128)(2,1)S(1)}, u32[]{:S(2)}, u32[]{:S(2)}) %collective-permute-start.4) | collective-permute-done | bytes 196640 | tf_op jit(solution)/shard_map/ppermute | solution.py:21
  34.9 1.3 collective-permute-start.14
  36.3 2.2 collective-permute-start.15
  38.5 1.5 collective-permute-start.16
  40.1 3.4 %collective-permute-start.12 = (bf16[4,4,48,512]{3,2,1,0:T(8,128)(2,1)}, bf16[4,4,48,512]{3,2,1,0:T(8,128)(2,1)}, u32[]{:S(2)}, u32[]{:S(2)}) collective-permute-start(bf16[4,4,48,512]{3,2,1,0:T(8,128)(2,1)} %bitcast_dynamic-update-slice_fusion.12), channel_id=1, source_target_pairs={{0,65},{1,0},{64,1},{65,64},{2,67},{3,2},{66,3},{67,66},{4,69},{5,... | collective-permute-start | bytes 2359304 | tf_op jit(solution)/shard_map/ppermute | solution.py:21
  43.5 2.0 broadcast.146.clone.1
  45.6 2.1 bitcast_dynamic-update-slice_fusion.3
  48.3 5.7 %all-to-all-start = ((f32[8,8,128]{2,1,0:T(8,128)}), f32[8,8,128]{2,1,0:T(8,128)S(1)}, u32[]{:S(2)}, u32[]{:S(2)}) async-start(f32[8,8,128]{2,1,0:T(8,128)} %broadcast_in_dim.98), calls=%async_computation | async-start | bytes 65536 | tf_op jit(solution)/shard_map/all_to_all | solution.py:227
  54.3 1.2 bitcast_dynamic-update-slice_fusion.7
  55.5 16.2 %all-to-all-done = f32[8,8,128]{2,1,0:T(8,128)S(1)} async-done(((f32[8,8,128]{2,1,0:T(8,128)}), f32[8,8,128]{2,1,0:T(8,128)S(1)}, u32[]{:S(2)}, u32[]{:S(2)}) %all-to-all-start) | async-done | bytes 32800 | tf_op jit(solution)/shard_map/all_to_all | solution.py:227
  71.9 3.2 %collective-permute-start.13 = (bf16[4,4,48,512]{3,2,1,0:T(8,128)(2,1)}, bf16[4,4,48,512]{3,2,1,0:T(8,128)(2,1)S(1)}, u32[]{:S(2)}, u32[]{:S(2)}) collective-permute-start(bf16[4,4,48,512]{3,2,1,0:T(8,128)(2,1)} %bitcast_dynamic-update-slice_fusion.12), channel_id=1, source_target_pairs={{0,64},{1,65},{64,0},{65,1},{2,66},{3,67},{66,2},{67,3},{4,68},{5,... | collective-permute-start | bytes 2359304 | tf_op jit(solution)/shard_map/ppermute | solution.py:21
  75.1 2.1 bitcast_dynamic-update-slice_fusion.2
  77.2 2.1 bitcast_dynamic-update-slice_fusion.1
  79.3 2.1 bitcast_dynamic-update-slice_fusion
  81.4 1.2 bitcast_dynamic-update-slice_fusion.6
  82.6 1.2 bitcast_dynamic-update-slice_fusion.5
  83.8 3.3 %copy-done.3 = bf16[4096,1002]{0,1:T(8,128)(2,1)S(1)} copy-done((bf16[4096,1002]{0,1:T(8,128)(2,1)S(1)}, bf16[4096,1002]{0,1:T(8,128)(2,1)}, u32[]{:S(2)}) %copy-start.3) | copy-done | bytes 8208408
  87.1 17.5 %shard_map.104 = (f32[1002,384]{1,0:T(8,128)S(1)}, f32[1002,384]{1,0:T(8,128)S(1)}, f32[8,384]{1,0:T(8,128)S(1)}) custom-call(s32[2]{0:T(128)S(1)} %pad_add_fusion.base_ref, s32[1,384]{1,0:T(1,128)S(1)} %convert_element_type.45.action_ref, bf16[4,2,2,4,48,512]{5,4,3,2,1,0:T(8,128)(2,1)} %bitcast.34.hidden_ref, bf16[1002,4096]{1,0:T(8,128)(2,1)S(1)} %bitcast.92, ...), custom_call_target="tpu_custom_call" | custom-call | flops 6304038912 | bytes 19562496 | tf_op jit(solution)/shard_map/pallas_call | solution.py:106
  104.7 4.4 %copy-done.4 = bf16[4096,1002]{0,1:T(8,128)(2,1)S(1)} copy-done((bf16[4096,1002]{0,1:T(8,128)(2,1)S(1)}, bf16[4096,1002]{0,1:T(8,128)(2,1)}, u32[]{:S(2)}) %copy-start.4) | copy-done | bytes 8208408
  109.1 17.7 %shard_map.103 = (f32[1002,384]{1,0:T(8,128)S(1)}, f32[1002,384]{1,0:T(8,128)S(1)}, f32[8,384]{1,0:T(8,128)S(1)}) custom-call(s32[2]{0:T(128)S(1)} %pad_add_fusion.base_ref, s32[1,384]{1,0:T(1,128)S(1)} %convert_element_type.45.action_ref, bf16[2,2,4,4,48,512]{5,4,3,2,1,0:T(8,128)(2,1)S(1)} %bitcast.87, bf16[1002,4096]{1,0:T(8,128)(2,1)S(1)} %bitcast.95, ...), custom_call_target="tpu_custom_call" | custom-call | flops 6304038912 | bytes 19562496 | tf_op jit(solution)/shard_map/pallas_call | solution.py:106
  126.8 1.1 copy-done.9
  127.9 1.2 copy-done.11
  130.1 6.3 %all-to-all-start.1 = ((f32[64,8,384]{2,1,0:T(8,128)}), f32[64,8,384]{2,1,0:T(8,128)}, u32[]{:S(2)}, u32[]{:S(2)}) async-start(f32[64,8,384]{2,1,0:T(8,128)} %broadcast_in_dim.107), calls=%async_computation.1 | async-start | bytes 1572864 | tf_op jit(solution)/shard_map/all_to_all | solution.py:244
  136.8 11.8 %all-to-all-done.1 = f32[64,8,384]{2,1,0:T(8,128)} async-done(((f32[64,8,384]{2,1,0:T(8,128)}), f32[64,8,384]{2,1,0:T(8,128)}, u32[]{:S(2)}, u32[]{:S(2)}) %all-to-all-start.1) | async-done | bytes 786464 | tf_op jit(solution)/shard_map/all_to_all | solution.py:244
  148.5 3.0 %fusion.36 = (f32[64,1,384]{2,1,0:T(1,128)S(1)}, f32[64,1,384]{2,1,0:T(1,128)S(1)}, f32[384]{0:T(512)S(1)}, f32[384]{0:T(512)S(1)}, f32[384]{0:T(512)S(1)}, /*in...) fusion(f32[64,8,384]{2,1,0:T(8,128)} %all-to-all-done.1), kind=kLoop, calls=%fused_computation.83 | loop fusion | flops 72576 | bytes 889344 | tf_op jit(solution)/shard_map/slice | solution.py:250
  151.9 1.4 copy-done.6
  153.2 1.4 copy-done.8
  154.6 1.4 copy-done.10
  156.0 1.4 copy-done.12
  157.4 13.3 %shard_map.105 = (bf16[1002,384]{1,0:T(8,128)(2,1)S(1)}, bf16[1002,384]{1,0:T(8,128)(2,1)S(1)}, bf16[8,8,48,512]{3,2,1,0:T(8,128)(2,1)S(1)}) custom-call(s32[2]{0:T(128)S(1)} %pad_add_fusion.base_ref, s32[1,384]{1,0:T(1,128)S(1)} %convert_element_type.45.action_ref, f32[8,384]{1,0:T(8,128)S(1)} %stack.42.vec_ref, f32[1002,384]{1,0:T(8,128)S(1)} %copy-done.10, ...), custom_call_target="tpu_custom_call" | custom-call | flops 6304038912 | bytes 19562496 | tf_op jit(solution)/shard_map/pallas_call | solution.py:154
  170.7 1.7 copy-done
  172.4 7.5 %shard_map.106 = bf16[1002,4096]{1,0:T(8,128)(2,1)} custom-call(bf16[1002,384]{1,0:T(8,128)(2,1)S(1)} %get-tuple-element.29.grad_ref, bf16[2,2,4,4,48,512]{5,4,3,2,1,0:T(8,128)(2,1)S(1)} %bitcast.88), custom_call_target="tpu_custom_call" | custom-call | flops 3152019456 | bytes 11354112 | tf_op jit(solution)/shard_map/pallas_call | solution.py:187
  180.0 6.1 %all-to-all-start.2 = ((bf16[64,48,512]{2,1,0:T(8,128)(2,1)}), bf16[64,48,512]{2,1,0:T(8,128)(2,1)}, u32[]{:S(2)}, u32[]{:S(2)}) async-start(bf16[64,48,512]{2,1,0:T(8,128)(2,1)} %bitcast.90), calls=%async_computation.2 | async-start | bytes 6291456 | tf_op jit(solution)/shard_map/all_to_all | solution.py:279
  187.0 6.0 %collective-permute-done.18 = f32[16,24]{1,0:T(8,128)S(1)} collective-permute-done((f32[16,24]{1,0:T(8,128)S(1)}, f32[16,24]{1,0:T(8,128)S(1)}, u32[]{:S(2)}, u32[]{:S(2)}) %collective-permute-start.18) | collective-permute-done | bytes 1568 | tf_op jit(solution)/shard_map/ppermute | solution.py:25
  193.5 34.6 %all-to-all-done.2 = bf16[64,48,512]{2,1,0:T(8,128)(2,1)} async-done(((bf16[64,48,512]{2,1,0:T(8,128)(2,1)}), bf16[64,48,512]{2,1,0:T(8,128)(2,1)}, u32[]{:S(2)}, u32[]{:S(2)}) %all-to-all-start.2) | async-done | bytes 3145760 | tf_op jit(solution)/shard_map/all_to_all | solution.py:279
  228.0 3.0 %reduce_sum.53 = bf16[48,512]{1,0:T(8,128)(2,1)} reduce(bf16[64,48,512]{2,1,0:T(8,128)(2,1)} %all-to-all-done.2, bf16[]{:T(256)} %constant.114.clone.1), dimensions={0}, to_apply=%region_5.6 | reduce | flops 1548288 | bytes 3194882 | tf_op jit(solution)/shard_map/reduce_sum | solution.py:280
  231.0 1.1 copy-done.2
  232.2 10.8 %shard_map.107 = bf16[1002,4096]{1,0:T(8,128)(2,1)} custom-call(bf16[1002,384]{1,0:T(8,128)(2,1)S(1)} %copy-done.2, bf16[2,2,4,4,48,512]{5,4,3,2,1,0:T(8,128)(2,1)S(1)} %bitcast.89, bf16[1002,4096]{1,0:T(8,128)(2,1)} %collective-permute-done.17.refs_0_), custom_call_target="tpu_custom_call" | custom-call | flops 3152019456 | bytes 19562496 | tf_op jit(solution)/shard_map/pallas_call | solution.py:187
  (91 shorter events, 16.9 us)
Async XLA Ops:
  0.6 34.2 %collective-permute-start.9 = (bf16[1002,4096]{1,0:T(8,128)(2,1)}, bf16[1002,4096]{1,0:T(8,128)(2,1)}, u32[]{:S(2)}, u32[]{:S(2)}) collective-permute-start(bf16[1002,4096]{1,0:T(8,128)(2,1)} %bitcast.93), channel_id=1, source_target_pairs={{0,8},{8,0},{1,9},{9,1},{2,10},{10,2},{3,11},{11,3},{4,12},{12,4},... | collective-permute-start | bytes 24625160 | tf_op jit(solution)/shard_map/ppermute | solution.py:25
  0.7 34.2 %collective-permute-start.10 = (bf16[1002,4096]{1,0:T(8,128)(2,1)}, bf16[1002,4096]{1,0:T(8,128)(2,1)}, u32[]{:S(2)}, u32[]{:S(2)}) collective-permute-start(bf16[1002,4096]{1,0:T(8,128)(2,1)} %bitcast.91), channel_id=1, source_target_pairs={{0,8},{8,0},{1,9},{9,1},{2,10},{10,2},{3,11},{11,3},{4,12},{12,4},... | collective-permute-start | bytes 24625160 | tf_op jit(solution)/shard_map/ppermute | solution.py:25
  2.1 9.6 %collective-permute-start = (bf16[2,48,512]{2,1,0:T(8,128)(2,1)S(1)}, bf16[2,48,512]{2,1,0:T(8,128)(2,1)S(1)}, u32[]{:S(2)}, u32[]{:S(2)}) collective-permute-start(bf16[2,48,512]{2,1,0:T(8,128)(2,1)S(1)} %pad_maximum_fusion), channel_id=1, source_target_pairs={{0,2},{2,4},{4,6},{6,0},{1,3},{3,5},{5,7},{7,1},{8,10},{10,12},{12... | collective-permute-start | bytes 294920 | tf_op jit(solution)/shard_map/ppermute | solution.py:21
  4.1 7.6 %collective-permute-start.1 = (bf16[2,48,512]{2,1,0:T(8,128)(2,1)S(1)}, bf16[2,48,512]{2,1,0:T(8,128)(2,1)S(1)}, u32[]{:S(2)}, u32[]{:S(2)}) collective-permute-start(bf16[2,48,512]{2,1,0:T(8,128)(2,1)S(1)} %pad_maximum_fusion), channel_id=1, source_target_pairs={{0,6},{2,0},{4,2},{6,4},{1,7},{3,1},{5,3},{7,5},{8,14},{10,8},{12,... | collective-permute-start | bytes 294920 | tf_op jit(solution)/shard_map/ppermute | solution.py:21
  6.3 6.3 %collective-permute-start.2 = (bf16[2,48,512]{2,1,0:T(8,128)(2,1)S(1)}, bf16[2,48,512]{2,1,0:T(8,128)(2,1)S(1)}, u32[]{:S(2)}, u32[]{:S(2)}) collective-permute-start(bf16[2,48,512]{2,1,0:T(8,128)(2,1)S(1)} %pad_maximum_fusion), channel_id=1, source_target_pairs={{0,4},{2,6},{4,0},{6,2},{1,5},{3,7},{5,1},{7,3},{8,12},{10,14},{12... | collective-permute-start | bytes 294920 | tf_op jit(solution)/shard_map/ppermute | solution.py:21
  12.6 8.6 %collective-permute-start.6 = (bf16[4,48,512]{2,1,0:T(8,128)(2,1)S(1)}, bf16[4,48,512]{2,1,0:T(8,128)(2,1)S(1)}, u32[]{:S(2)}, u32[]{:S(2)}) collective-permute-start(bf16[4,48,512]{2,1,0:T(8,128)(2,1)S(1)} %get-tuple-element.41), channel_id=1, source_target_pairs={{0,1},{1,64},{64,65},{65,0},{2,3},{3,66},{66,67},{67,2},{4,5},{5,6... | collective-permute-start | bytes 589832 | tf_op jit(solution)/shard_map/ppermute | solution.py:21
  14.3 9.3 %collective-permute-start.7 = (bf16[4,48,512]{2,1,0:T(8,128)(2,1)S(1)}, bf16[4,48,512]{2,1,0:T(8,128)(2,1)S(1)}, u32[]{:S(2)}, u32[]{:S(2)}) collective-permute-start(bf16[4,48,512]{2,1,0:T(8,128)(2,1)S(1)} %get-tuple-element.41), channel_id=1, source_target_pairs={{0,65},{1,0},{64,1},{65,64},{2,67},{3,2},{66,3},{67,66},{4,69},{5,... | collective-permute-start | bytes 589832 | tf_op jit(solution)/shard_map/ppermute | solution.py:21
  15.9 11.1 %collective-permute-start.8 = (bf16[4,48,512]{2,1,0:T(8,128)(2,1)S(1)}, bf16[4,48,512]{2,1,0:T(8,128)(2,1)S(1)}, u32[]{:S(2)}, u32[]{:S(2)}) collective-permute-start(bf16[4,48,512]{2,1,0:T(8,128)(2,1)S(1)} %get-tuple-element.41), channel_id=1, source_target_pairs={{0,64},{1,65},{64,0},{65,1},{2,66},{3,67},{66,2},{67,3},{4,68},{5,... | collective-permute-start | bytes 589832 | tf_op jit(solution)/shard_map/ppermute | solution.py:21
  21.3 7.8 %collective-permute-start.3 = (bf16[4,48,512]{2,1,0:T(8,128)(2,1)S(1)}, bf16[4,48,512]{2,1,0:T(8,128)(2,1)S(1)}, u32[]{:S(2)}, u32[]{:S(2)}) collective-permute-start(bf16[4,48,512]{2,1,0:T(8,128)(2,1)S(1)} %get-tuple-element.42), channel_id=1, source_target_pairs={{0,16},{16,32},{32,48},{48,0},{1,17},{17,33},{33,49},{49,1},{2,18}... | collective-permute-start | bytes 589832 | tf_op jit(solution)/shard_map/ppermute | solution.py:21
  23.5 9.9 %collective-permute-start.4 = (bf16[4,48,512]{2,1,0:T(8,128)(2,1)S(1)}, bf16[4,48,512]{2,1,0:T(8,128)(2,1)S(1)}, u32[]{:S(2)}, u32[]{:S(2)}) collective-permute-start(bf16[4,48,512]{2,1,0:T(8,128)(2,1)S(1)} %get-tuple-element.42), channel_id=1, source_target_pairs={{0,48},{16,0},{32,16},{48,32},{1,49},{17,1},{33,17},{49,33},{2,50}... | collective-permute-start | bytes 589832 | tf_op jit(solution)/shard_map/ppermute | solution.py:21
  27.0 7.2 %collective-permute-start.5 = (bf16[4,48,512]{2,1,0:T(8,128)(2,1)S(1)}, bf16[4,48,512]{2,1,0:T(8,128)(2,1)S(1)}, u32[]{:S(2)}, u32[]{:S(2)}) collective-permute-start(bf16[4,48,512]{2,1,0:T(8,128)(2,1)S(1)} %get-tuple-element.42), channel_id=1, source_target_pairs={{0,32},{16,48},{32,0},{48,16},{1,33},{17,49},{33,1},{49,17},{2,34}... | collective-permute-start | bytes 589832 | tf_op jit(solution)/shard_map/ppermute | solution.py:21
  34.9 37.0 %collective-permute-start.14 = (bf16[4,4,48,512]{3,2,1,0:T(8,128)(2,1)}, bf16[4,4,48,512]{3,2,1,0:T(8,128)(2,1)}, u32[]{:S(2)}, u32[]{:S(2)}) collective-permute-start(bf16[4,4,48,512]{3,2,1,0:T(8,128)(2,1)} %bitcast_dynamic-update-slice_fusion.8), channel_id=1, source_target_pairs={{0,16},{16,32},{32,48},{48,0},{1,17},{17,33},{33,49},{49,1},{2,18}... | collective-permute-start | bytes 2359304 | tf_op jit(solution)/shard_map/ppermute | solution.py:21
  36.3 40.9 %collective-permute-start.15 = (bf16[4,4,48,512]{3,2,1,0:T(8,128)(2,1)}, bf16[4,4,48,512]{3,2,1,0:T(8,128)(2,1)}, u32[]{:S(2)}, u32[]{:S(2)}) collective-permute-start(bf16[4,4,48,512]{3,2,1,0:T(8,128)(2,1)} %bitcast_dynamic-update-slice_fusion.8), channel_id=1, source_target_pairs={{0,48},{16,0},{32,16},{48,32},{1,49},{17,1},{33,17},{49,33},{2,50}... | collective-permute-start | bytes 2359304 | tf_op jit(solution)/shard_map/ppermute | solution.py:21
  38.5 40.7 %collective-permute-start.16 = (bf16[4,4,48,512]{3,2,1,0:T(8,128)(2,1)}, bf16[4,4,48,512]{3,2,1,0:T(8,128)(2,1)}, u32[]{:S(2)}, u32[]{:S(2)}) collective-permute-start(bf16[4,4,48,512]{3,2,1,0:T(8,128)(2,1)} %bitcast_dynamic-update-slice_fusion.8), channel_id=1, source_target_pairs={{0,32},{16,48},{32,0},{48,16},{1,33},{17,49},{33,1},{49,17},{2,34}... | collective-permute-start | bytes 2359304 | tf_op jit(solution)/shard_map/ppermute | solution.py:21
  40.1 41.3 %collective-permute-start.11 = (bf16[4,4,48,512]{3,2,1,0:T(8,128)(2,1)}, bf16[4,4,48,512]{3,2,1,0:T(8,128)(2,1)}, u32[]{:S(2)}, u32[]{:S(2)}) collective-permute-start(bf16[4,4,48,512]{3,2,1,0:T(8,128)(2,1)} %bitcast_dynamic-update-slice_fusion.12), channel_id=1, source_target_pairs={{0,1},{1,64},{64,65},{65,0},{2,3},{3,66},{66,67},{67,2},{4,5},{5,6... | collective-permute-start | bytes 2359304 | tf_op jit(solution)/shard_map/ppermute | solution.py:21
  40.1 42.5 %collective-permute-start.12 = (bf16[4,4,48,512]{3,2,1,0:T(8,128)(2,1)}, bf16[4,4,48,512]{3,2,1,0:T(8,128)(2,1)}, u32[]{:S(2)}, u32[]{:S(2)}) collective-permute-start(bf16[4,4,48,512]{3,2,1,0:T(8,128)(2,1)} %bitcast_dynamic-update-slice_fusion.12), channel_id=1, source_target_pairs={{0,65},{1,0},{64,1},{65,64},{2,67},{3,2},{66,3},{67,66},{4,69},{5,... | collective-permute-start | bytes 2359304 | tf_op jit(solution)/shard_map/ppermute | solution.py:21
  48.3 23.5 %all-to-all-start = ((f32[8,8,128]{2,1,0:T(8,128)}), f32[8,8,128]{2,1,0:T(8,128)S(1)}, u32[]{:S(2)}, u32[]{:S(2)}) async-start(f32[8,8,128]{2,1,0:T(8,128)} %broadcast_in_dim.98), calls=%async_computation | async-start | bytes 65536 | tf_op jit(solution)/shard_map/all_to_all | solution.py:227
  71.9 32.8 %collective-permute-start.13 = (bf16[4,4,48,512]{3,2,1,0:T(8,128)(2,1)}, bf16[4,4,48,512]{3,2,1,0:T(8,128)(2,1)S(1)}, u32[]{:S(2)}, u32[]{:S(2)}) collective-permute-start(bf16[4,4,48,512]{3,2,1,0:T(8,128)(2,1)} %bitcast_dynamic-update-slice_fusion.12), channel_id=1, source_target_pairs={{0,64},{1,65},{64,0},{65,1},{2,66},{3,67},{66,2},{67,3},{4,68},{5,... | collective-permute-start | bytes 2359304 | tf_op jit(solution)/shard_map/ppermute | solution.py:21
  83.8 3.3 %copy-start.3 = (bf16[4096,1002]{0,1:T(8,128)(2,1)S(1)}, bf16[4096,1002]{0,1:T(8,128)(2,1)}, u32[]{:S(2)}) copy-start(bf16[4096,1002]{0,1:T(8,128)(2,1)} %param.12) | copy-start | bytes 24625156
  104.6 22.1 %copy-start.5 = (f32[1002,384]{1,0:T(8,128)}, f32[1002,384]{1,0:T(8,128)S(1)}, u32[]{:S(2)}) copy-start(f32[1002,384]{1,0:T(8,128)S(1)} %get-tuple-element.26.tq_own) | copy-start | bytes 4617220
  104.6 22.1 %copy-start.7 = (f32[1002,384]{1,0:T(8,128)}, f32[1002,384]{1,0:T(8,128)S(1)}, u32[]{:S(2)}) copy-start(f32[1002,384]{1,0:T(8,128)S(1)} %get-tuple-element.27.tq_sib) | copy-start | bytes 4617220
  104.7 4.4 %copy-start.4 = (bf16[4096,1002]{0,1:T(8,128)(2,1)S(1)}, bf16[4096,1002]{0,1:T(8,128)(2,1)}, u32[]{:S(2)}) copy-start(bf16[4096,1002]{0,1:T(8,128)(2,1)} %param.11) | copy-start | bytes 24625156
  126.8 1.1 copy-start.9
  127.9 1.2 copy-start.11
  130.1 18.4 %all-to-all-start.1 = ((f32[64,8,384]{2,1,0:T(8,128)}), f32[64,8,384]{2,1,0:T(8,128)}, u32[]{:S(2)}, u32[]{:S(2)}) async-start(f32[64,8,384]{2,1,0:T(8,128)} %broadcast_in_dim.107), calls=%async_computation.1 | async-start | bytes 1572864 | tf_op jit(solution)/shard_map/all_to_all | solution.py:244
  151.8 1.4 copy-start.6
  153.2 1.4 copy-start.8
  154.6 1.4 copy-start.10
  156.0 1.4 copy-start.12
  170.7 1.7 copy-start
  172.4 7.5 %copy-start.1 = (bf16[1002,384]{1,0:T(8,128)(2,1)}, bf16[1002,384]{1,0:T(8,128)(2,1)S(1)}, u32[]{:S(2)}) copy-start(bf16[1002,384]{1,0:T(8,128)(2,1)S(1)} %get-tuple-element.28.grad_ref) | copy-start | bytes 2308612
  180.0 51.1 %collective-permute-start.17 = (bf16[1002,4096]{1,0:T(8,128)(2,1)}, bf16[1002,4096]{1,0:T(8,128)(2,1)}, u32[]{:S(2)}, u32[]{:S(2)}) collective-permute-start(bf16[1002,4096]{1,0:T(8,128)(2,1)} %shard_map.106), channel_id=1, source_target_pairs={{0,8},{8,0},{1,9},{9,1},{2,10},{10,2},{3,11},{11,3},{4,12},{12,4},... | collective-permute-start | bytes 24625160 | tf_op jit(solution)/shard_map/ppermute | solution.py:25
  180.0 48.1 %all-to-all-start.2 = ((bf16[64,48,512]{2,1,0:T(8,128)(2,1)}), bf16[64,48,512]{2,1,0:T(8,128)(2,1)}, u32[]{:S(2)}, u32[]{:S(2)}) async-start(bf16[64,48,512]{2,1,0:T(8,128)(2,1)} %bitcast.90), calls=%async_computation.2 | async-start | bytes 6291456 | tf_op jit(solution)/shard_map/all_to_all | solution.py:279
  186.7 6.2 %collective-permute-start.18 = (f32[16,24]{1,0:T(8,128)S(1)}, f32[16,24]{1,0:T(8,128)S(1)}, u32[]{:S(2)}, u32[]{:S(2)}) collective-permute-start(f32[16,24]{1,0:T(8,128)S(1)} %fusion.8), channel_id=1, source_target_pairs={{0,8},{8,0},{1,9},{9,1},{2,10},{10,2},{3,11},{11,3},{4,12},{12,4},... | collective-permute-start | bytes 4616 | tf_op jit(solution)/shard_map/ppermute | solution.py:25
  231.0 1.1 copy-start.2

commit v2 on v1

v2 whole, which is shorter than its diff:
```python
import functools

import jax
import jax.numpy as jnp
from jax import lax
from jax.experimental import pallas as pl
from jax.experimental.pallas import tpu as pltpu
from jax.sharding import Mesh, PartitionSpec as P

temper = 1.0
discount = 0.99
kl_weight = 10.0

DP = ("yh", "x", "c")
TENSOR = ("z", "yl")
PLANE = ("yh", "x", "z", "yl")
Y = ("yh", "yl")


def shift(v, axis, by):
    return lax.ppermute(v, axis, [(i, (i + by) % 4) for i in range(4)])


def swap_cores(v):
    return lax.ppermute(v, "c", [(0, 1), (1, 0)])


def ring_blocks(v, axis):
    ahead, back, across = (shift(v, axis, by) for by in (1, 3, 2))
    return v, ahead, across, back


def gather_ring(v, axis):
    me = lax.axis_index(axis)
    out = jnp.zeros((4,) + v.shape, v.dtype)
    for by, block in enumerate(ring_blocks(v, axis)):
        out = lax.dynamic_update_index_in_dim(out, block, (me - by) & 3, 0)
    return out


VMEM_LIMIT = 60 * 1024 * 1024
NT = (((1,), (1,)), ((), ()))
NN = (((1,), (0,)), ((), ()))


def whole(shape):
    return pl.BlockSpec(shape, lambda j: (0,) * len(shape))


def cost(flops, nbytes, exps=0):
    return pl.CostEstimate(flops=flops, bytes_accessed=nbytes, transcendentals=exps)


def columns_of(ref):
    turned = jnp.concatenate([ref[...]] * 16, axis=0).T
    return [turned[:, k : k + 1] for k in range(8)]


def place_blocks(x_ring, ids_ref, blocks, out_ref):
    rows, feats = blocks[0].shape[-2:]
    for by, block in enumerate(blocks):
        place = (ids_ref[2] - by) & 3
        if x_ring:
            for y in range(4):
                at = pl.multiple_of(((y // 2) * 4 + place) * rows, rows)
                out_ref[pl.ds(at, rows), (y % 2) * feats : (y % 2 + 1) * feats] = block[y]
        else:
            at = pl.multiple_of((place // 2) * 4 * rows, 4 * rows)
            lane = pl.multiple_of((place % 2) * feats, feats)
            out_ref[pl.ds(at, 4 * rows), pl.ds(lane, feats)] = block[...].reshape(4 * rows, feats)


def q_kernel(x_ring, ids_ref, vec_ref, b0, b1, b2, b3, own_ref, sib_ref, e_own, e_sib, stats_ref, hidden_ref):
    j = pl.program_id(0)
    place_blocks(x_ring, ids_ref, (b0, b1, b2, b3), hidden_ref)
    for head_ref, q_ref in ((own_ref, e_own), (sib_ref, e_sib)):
        part = lax.dot_general(hidden_ref[...], head_ref[...], NT, preferred_element_type=jnp.float32)

        @pl.when(j == 0)
        def _():
            q_ref[...] = part

        @pl.when(j > 0)
        def _():
            q_ref[...] += part

    @pl.when(j == pl.num_programs(0) - 1)
    def _():
        peak = jnp.maximum(
            jnp.max(e_own[...], axis=1, keepdims=True), jnp.max(e_sib[...], axis=1, keepdims=True)
        )
        total = jnp.zeros_like(peak)
        picked = jnp.zeros_like(peak)
        if not x_ring:
            action = columns_of(vec_ref)[0].astype(jnp.int32)
            ids = lax.broadcasted_iota(jnp.int32, e_own.shape, 1)
        for k, q_ref in enumerate((e_own, e_sib)):
            q = q_ref[...]
            if not x_ring:
                hit = ids == action - ids_ref[k]
                picked += jnp.sum(jnp.where(hit, q, 0.0), axis=1, keepdims=True)
            expo = jnp.exp((q - peak) / temper)
            total += jnp.sum(expo, axis=1, keepdims=True)
            q_ref[...] = expo
        lane = lax.broadcasted_iota(jnp.int32, (peak.shape[0], 128), 1)
        first = 2 if x_ring else 0
        table = jnp.where(lane == first, peak, jnp.where(lane == first + 1, total, 0.0))
        if not x_ring:
            table = jnp.where(lane == 4, picked, table)
        stats_ref[...] = table.T[:8]


def q_values(blocks, heads, ids, vec, x_ring, rows):
    width, feats_all = heads[0].shape
    feats = blocks[0].shape[-1]
    tokens = vec.shape[1]
    block_spec = pl.BlockSpec((4, rows, feats), lambda j: (0, j, 0))
    head_spec = pl.BlockSpec((width, 2 * feats), lambda j: (0, j))
    hidden_spec = pl.BlockSpec((tokens, 2 * feats), lambda j: (0, j))
    q_shape = jax.ShapeDtypeStruct((tokens, width), jnp.float32)
    stats_shape = jax.ShapeDtypeStruct((8, tokens), jnp.float32)
    hidden_shape = jax.ShapeDtypeStruct((tokens, feats_all), jnp.bfloat16)
    outs = [q_shape, q_shape, stats_shape]
    out_specs = [whole(o.shape) for o in outs]
    scratch = [pltpu.VMEM((tokens, 2 * feats), jnp.bfloat16)]
    if not x_ring:
        outs, out_specs, scratch = outs + [hidden_shape], out_specs + [hidden_spec], []
    return pl.pallas_call(
        functools.partial(q_kernel, x_ring),
        grid=(feats_all // (2 * feats),),
        in_specs=[pl.BlockSpec(memory_space=pltpu.SMEM), whole(vec.shape)] + [block_spec] * 4 + [head_spec] * 2,
        out_specs=out_specs,
        out_shape=outs,
        scratch_shapes=scratch,
        compiler_params=pltpu.CompilerParams(vmem_limit_bytes=VMEM_LIMIT),
        cost_estimate=cost(
            4 * tokens * width * feats_all, 4 * width * feats_all + 2 * tokens * feats_all, 2 * tokens * width
        ),
    )(ids, vec, *blocks, *heads)


def grad_kernel(
    scale, ids_ref, vec_ref, le_own, le_sib, te_own, te_sib, own_ref, sib_ref,
    turned_own, turned_sib, part_ref, g_own, g_sib,
):
    @pl.when(pl.program_id(0) == 0)
    def _():
        action, learn_gain, target_gain, delta = columns_of(vec_ref)[:4]
        action = action.astype(jnp.int32)
        ids = lax.broadcasted_iota(jnp.int32, le_own.shape, 1)
        for k, (le, te, out, turned) in enumerate(
            ((le_own, te_own, g_own, turned_own), (le_sib, te_sib, g_sib, turned_sib))
        ):
            hit = ids == action - ids_ref[k]
            both = le[...] * learn_gain - te[...] * target_gain
            grad = (jnp.where(hit, delta, 0.0) + both / temper) * scale
            out[...] = grad.astype(jnp.bfloat16)
            turned[...] = grad.T.astype(jnp.bfloat16)

    part = lax.dot_general(g_own[...], own_ref[...], NN, preferred_element_type=jnp.float32)
    part += lax.dot_general(g_sib[...], sib_ref[...], NN, preferred_element_type=jnp.float32)
    part = part.astype(jnp.bfloat16)
    groups, _, rows, feats = part_ref.shape
    for k in range(2):
        part_ref[:, k] = part[:, k * feats : (k + 1) * feats].reshape(groups, rows, feats)


def gradients(learn_e, target_e, heads, ids, vec, rows, feats, traj_total):
    width, feats_all = heads[0].shape
    tokens = vec.shape[1]
    groups = tokens // rows
    head_spec = pl.BlockSpec((width, 2 * feats), lambda j: (0, j))
    g_shape = jax.ShapeDtypeStruct((width, tokens), jnp.bfloat16)
    return pl.pallas_call(
        functools.partial(grad_kernel, 1.0 / traj_total),
        grid=(feats_all // (2 * feats),),
        in_specs=[pl.BlockSpec(memory_space=pltpu.SMEM), whole(vec.shape)]
        + [whole((tokens, width))] * 4
        + [head_spec] * 2,
        out_specs=[whole((width, tokens))] * 2
        + [pl.BlockSpec((groups, 2, rows, feats), lambda j: (0, j, 0, 0))],
        out_shape=[g_shape, g_shape]
        + [jax.ShapeDtypeStruct((groups, feats_all // feats, rows, feats), jnp.bfloat16)],
        scratch_shapes=[pltpu.VMEM((tokens, width), jnp.bfloat16)] * 2,
        compiler_params=pltpu.CompilerParams(vmem_limit_bytes=VMEM_LIMIT),
        cost_estimate=cost(
            4 * tokens * width * feats_all, 4 * width * feats_all + 2 * tokens * feats_all, 0
        ),
    )(ids, vec, *learn_e, *target_e, *heads)


def head_kernel(grad_a, grad_b, hidden_a, hidden_b, out_ref):
    total = lax.dot_general(grad_a[...], hidden_a[...], NN, preferred_element_type=jnp.float32)
    total += lax.dot_general(grad_b[...], hidden_b[...], NN, preferred_element_type=jnp.float32)
    out_ref[...] = total.astype(jnp.bfloat16)


def head_gradient(grads, hiddens):
    width, tokens = grads[0].shape
    feats_all = hiddens[0].shape[1]
    block = feats_all // 4
    return pl.pallas_call(
        head_kernel,
        grid=(4,),
        in_specs=[whole((width, tokens))] * 2 + [pl.BlockSpec((tokens, block), lambda j: (0, j))] * 2,
        out_specs=pl.BlockSpec((width, block), lambda j: (0, j)),
        out_shape=jax.ShapeDtypeStruct((width, feats_all), jnp.bfloat16),
        compiler_params=pltpu.CompilerParams(vmem_limit_bytes=VMEM_LIMIT),
        cost_estimate=cost(4 * tokens * width * feats_all, (2 * width + 4 * tokens) * feats_all),
    )(*grads, *hiddens)


def shards(learn_hidden, target_hidden, reward, learn_head, target_head, action, traj_len, owner):
    f32, bf16 = jnp.float32, jnp.bfloat16
    rows, feats = learn_hidden.shape
    width = learn_head.shape[1]
    trajs = traj_len.shape[0]
    tokens = rows * 8
    seq_len = rows // trajs
    traj_total = trajs * 16

    learn_head, target_head = learn_head.T, target_head.T
    learn_sib, target_sib = swap_cores(learn_head), swap_cores(target_head)

    extra = [action & 255, (action >> 8) & 255, action >> 16, reward, traj_len, owner]
    extra = jnp.concatenate([v.astype(bf16) for v in extra])
    extra = jnp.pad(extra[None], ((0, 15), (0, feats - extra.shape[0])))

    both = gather_ring(jnp.stack([learn_hidden, target_hidden]), "z")
    learn = gather_ring(jnp.concatenate([both[:, 0].reshape(4 * rows, feats), extra]), "x")
    target = gather_ring(both[:, 1], Y)
    learn, target, learn_sib, target_sib = lax.optimization_barrier(
        (learn, target, learn_sib, target_sib)
    )
    learn_blocks = ring_blocks(learn, Y)
    target_blocks = ring_blocks(target.reshape(4, 4 * rows, feats), "x")
    learn_heads, target_heads = (learn_head, learn_sib), (target_head, target_sib)

    mine, other = (learn_blocks[by][:, 4 * rows].astype(f32) for by in (0, 2))
    lower = lax.axis_index("yh") == 0
    small = jnp.concatenate([jnp.where(lower, mine, other), jnp.where(lower, other, mine)])

    def field(at, size):
        return small[:, at : at + size].reshape(8 * size)

    action_all = field(0, rows) + 256.0 * field(rows, rows) + 65536.0 * field(2 * rows, rows)
    reward_all = field(3 * rows, rows)
    length_all = field(4 * rows, trajs).astype(jnp.int32)
    owner_all = field(4 * rows + trajs, trajs).astype(jnp.int32)

    core = lax.axis_index("c")
    dp = lax.axis_index(DP)
    tensor = lax.axis_index(TENSOR)
    bases = [((dp + (1 - 2 * core) * k) * 8 + tensor) * width for k in (0, 1)]
    learn_ids = jnp.stack(bases + [lax.axis_index(Y)])
    target_ids = jnp.stack(bases + [lax.axis_index("x")])

    zeros = jnp.zeros((8, tokens), f32)
    *learn_e, learn_stats, learn = q_values(learn_blocks, learn_heads, learn_ids, zeros.at[0].set(action_all), False, rows)
    *target_e, target_stats = q_values(target_blocks, target_heads, target_ids, zeros, True, rows)

    packed = learn_stats + target_stats
    packed = lax.all_to_all(
        jnp.broadcast_to(packed[None], (64,) + packed.shape), PLANE, 0, 0, tiled=True
    )
    learn_max = jnp.max(packed[:, 0], axis=0)
    target_max = jnp.max(packed[:, 2], axis=0)
    learn_sum = jnp.sum(packed[:, 1] * jnp.exp((packed[:, 0] - learn_max) / temper), axis=0)
    target_sum = jnp.sum(packed[:, 3] * jnp.exp((packed[:, 2] - target_max) / temper), axis=0)
    picked = jnp.sum(packed[:, 4], axis=0)

    target_value = target_max + temper * jnp.log(target_sum)
    offset = jnp.arange(tokens, dtype=jnp.int32) % seq_len
    lengths = jnp.repeat(length_all, seq_len)
    live = (offset < lengths).astype(f32)
    follow = (offset + 1 < lengths).astype(f32)
    shifted = jnp.concatenate([target_value[1:], jnp.zeros((1,), f32)])
    target_y = reward_all + discount * follow * shifted
    delta = live * (picked - target_y)

    vec = jnp.stack(
        [
            action_all,
            kl_weight * live * jnp.exp((learn_stats[0] - learn_max) / temper) / learn_sum,
            kl_weight * live * jnp.exp((target_stats[2] - target_max) / temper) / target_sum,
            delta,
        ]
    )
    vec = jnp.concatenate([vec, jnp.zeros_like(vec)])
    grad_own, grad_sib, partial = gradients(
        learn_e, target_e, learn_heads, learn_ids, vec, rows, feats, traj_total
    )

    partial = lax.all_to_all(partial.reshape(64, rows, feats), PLANE, 0, 0, tiled=True)
    head_grad = head_gradient((grad_own, swap_cores(grad_sib)), (learn, swap_cores(learn)))
    partial, head_grad = lax.optimization_barrier((partial, head_grad))
    hidden_grad = jnp.sum(partial.astype(f32), axis=0).astype(bf16)
    head_grad = head_grad.T

    magnitude = jnp.abs(delta).reshape(8 * trajs, seq_len)
    owner_table = (jnp.arange(16, dtype=jnp.int32)[:, None] == owner_all[None, :]).astype(f32)
    sums = jnp.dot(owner_table, magnitude, precision=lax.Precision.HIGHEST)
    sums = sums + swap_cores(sums)
    priority = lax.dynamic_slice_in_dim(sums, dp, 1, 0)
    return (head_grad, hidden_grad, priority)


def solution(mesh):
    fine = Mesh(mesh.devices.reshape(2, 4, 2, 4, 2), ("yh", "x", "c", "z", "yl"))
    vocab = P(None, DP + TENSOR)
    return jax.shard_map(
        shards,
        mesh=fine,
        in_specs=(P(DP, TENSOR), P(DP, TENSOR), P(DP), vocab, vocab, P(DP), P(DP), P(DP)),
        out_specs=(vocab, P(DP, TENSOR), P(DP, None)),
        check_vma=False,
    )
```

time: 244 us -> 198 us (0.81)
  local copies, waits for them, and re-layouts: 42.9 us -> 6.24 us
  waiting for transfers between devices: 73.2 us -> 88.2 us
  starting transfers between devices: 47.6 us -> 36 us
  Pallas kernels: 66.7 us -> 57.1 us
  other arithmetic: 11.4 us -> 8.71 us
    ppermute x15, waiting for transfers between devices: 4.66 us -> 50.2 us  [shift(): return lax.ppermute(v, axis, [(i, (i + by) % 4) for i in range(4)])]
    unnamed x26 -> x9, local copies, waits for them, and re-layouts: 18.5 us -> 0.87 us
    dynamic_update_slice x19 -> x10, local copies, waits for them, and re-layouts: 17.6 us -> 0.17 us  [gather_ring(): out = lax.dynamic_update_index_in_dim(out, block, me - by & 3, 0)]
    all_to_all x1 -> x0, waiting for transfers between devices: 16.2 us -> none  [shards(): lax.all_to_all(jnp.broadcast_to(small[None, None], (8, 8, 128)), ('yh', '...]
    all_to_all x1, waiting for transfers between devices: 34.6 us -> 23 us  [shards(): lax.all_to_all(partial.reshape(64, rows, feats), PLANE, 0, 0, tiled=True)]
    pallas_call x5 -> x4, Pallas kernels: 66.7 us -> 57.1 us  [the longest x2 30.1 us: q_values(): pl.pallas_call(functools.partial(q_kernel, x_ring), grid=(feats_all // (2...]
    ppermute x15, starting transfers between devices: 28.7 us -> 22.8 us  [shift(): return lax.ppermute(v, axis, [(i, (i + by) % 4) for i in range(4)])]
    all_to_all x1 -> x0, starting transfers between devices: 5.7 us -> none  [shards(): lax.all_to_all(jnp.broadcast_to(small[None, None], (8, 8, 128)), ('yh', '...]
  transfers between devices with their start and end apart: 22 -> 22, of which waited for: 8 -> 7; matrix products, arithmetic and copies ran while one was open for 13% -> 6% of each run, Pallas kernels for 7% -> 21%
where the time goes in v2:
time: 198 us; the launch traced here: 197 us
  waiting for transfers between devices  88.2 us (45%)
  Pallas kernels  57.1 us (29%)
  starting transfers between devices  36 us (18%)
  other arithmetic  8.71 us (4%)
  local copies, waits for them, and re-layouts  6.24 us (3%)
    ppermute x15, waiting for transfers between devices, shift(): return lax.ppermute(v, axis, [(i, (i + by) % 4) for i in range(4)])  50.2 us
    pallas_call x2, Pallas kernels, q_values(): pl.pallas_call(functools.partial(q_kernel, x_ring), grid=(feats_all // (2...  30.1 us
    all_to_all x1, waiting for transfers between devices, shards(): lax.all_to_all(partial.reshape(64, rows, feats), PLANE, 0, 0, tiled=True)  23 us
    ppermute x15, starting transfers between devices, shift(): return lax.ppermute(v, axis, [(i, (i + by) % 4) for i in range(4)])  22.8 us
    pallas_call x1, Pallas kernels, gradients(): pl.pallas_call(functools.partial(grad_kernel, 1.0 / traj_total), grid=(fe...  14.5 us
    all_to_all x1, waiting for transfers between devices, shards(): lax.all_to_all(jnp.broadcast_to(packed[None], (64,) + packed.shape), PLAN...  13.9 us
    pallas_call x1, Pallas kernels, head_gradient(): pl.pallas_call(head_kernel, grid=(4,), in_specs=[whole((width, tokens))]...  12.5 us
    all_to_all x1, starting transfers between devices, shards(): lax.all_to_all(partial.reshape(64, rows, feats), PLANE, 0, 0, tiled=True)  5.9 us
  transfers between devices with their start and end apart: 22, of which 7 were waited for; matrix products, arithmetic and copies ran while one was open for 6% of the time, Pallas kernels for 21%

profile of v2, /device:TPU:0, one launch (start us, length us, event | category | flops | bytes accessed | tf_op | source)
XLA Modules:
  0.0 197.5 jit_solution(2337806424656807158)
XLA Ops:
  0.7 0.5 collective-permute-start.10
  1.2 0.8 pad_maximum_fusion
  2.1 4.0 %collective-permute-start.1 = (bf16[2,48,512]{2,1,0:T(8,128)(2,1)S(1)}, bf16[2,48,512]{2,1,0:T(8,128)(2,1)S(1)}, u32[]{:S(2)}, u32[]{:S(2)}) collective-permute-start(bf16[2,48,512]{2,1,0:T(8,128)(2,1)S(1)} %pad_maximum_fusion), channel_id=1, source_target_pairs={{0,4},{2,6},{4,0},{6,2},{1,5},{3,7},{5,1},{7,3},{8,12},{10,14},{12... | collective-permute-start | bytes 294920 | tf_op jit(solution)/shard_map/ppermute | solution.py:21
  6.1 1.0 collective-permute-start
  7.1 2.2 %collective-permute-start.2 = (bf16[2,48,512]{2,1,0:T(8,128)(2,1)S(1)}, bf16[2,48,512]{2,1,0:T(8,128)(2,1)S(1)}, u32[]{:S(2)}, u32[]{:S(2)}) collective-permute-start(bf16[2,48,512]{2,1,0:T(8,128)(2,1)S(1)} %pad_maximum_fusion), channel_id=1, source_target_pairs={{0,6},{2,0},{4,2},{6,4},{1,7},{3,1},{5,3},{7,5},{8,14},{10,8},{12,... | collective-permute-start | bytes 294920 | tf_op jit(solution)/shard_map/ppermute | solution.py:21
  9.3 0.7 convert_element_type.49
  10.0 0.7 convert_element_type.50
  10.6 0.7 shift-right-arithmetic_convert_fusion
  11.3 0.8 concatenate.30
  12.1 0.8 bitcast_dynamic-update-slice_fusion.11
  13.1 3.1 %collective-permute-start.8 = (bf16[4,48,512]{2,1,0:T(8,128)(2,1)S(1)}, bf16[4,48,512]{2,1,0:T(8,128)(2,1)S(1)}, u32[]{:S(2)}, u32[]{:S(2)}) collective-permute-start(bf16[4,48,512]{2,1,0:T(8,128)(2,1)S(1)} %get-tuple-element.57), channel_id=1, source_target_pairs={{0,65},{1,0},{64,1},{65,64},{2,67},{3,2},{66,3},{67,66},{4,69},{5,... | collective-permute-start | bytes 589832 | tf_op jit(solution)/shard_map/ppermute | solution.py:21
  16.2 0.6 collective-permute-start.7
  16.8 1.0 collective-permute-start.6
  18.0 9.7 %collective-permute-done.6 = bf16[4,48,512]{2,1,0:T(8,128)(2,1)S(1)} collective-permute-done((bf16[4,48,512]{2,1,0:T(8,128)(2,1)S(1)}, bf16[4,48,512]{2,1,0:T(8,128)(2,1)S(1)}, u32[]{:S(2)}, u32[]{:S(2)}) %collective-permute-start.6) | collective-permute-done | bytes 196640 | tf_op jit(solution)/shard_map/ppermute | solution.py:21
  27.7 3.0 %collective-permute-start.4 = (bf16[208,512]{1,0:T(8,128)(2,1)S(1)}, bf16[208,512]{1,0:T(8,128)(2,1)S(1)}, u32[]{:S(2)}, u32[]{:S(2)}) collective-permute-start(bf16[208,512]{1,0:T(8,128)(2,1)S(1)} %fusion.1), channel_id=1, source_target_pairs={{0,32},{16,48},{32,0},{48,16},{1,33},{17,49},{33,1},{49,17},{2,34}... | collective-permute-start | bytes 638984 | tf_op jit(solution)/shard_map/ppermute | solution.py:21
  30.7 0.7 collective-permute-start.3
  31.4 2.7 %collective-permute-start.5 = (bf16[208,512]{1,0:T(8,128)(2,1)S(1)}, bf16[208,512]{1,0:T(8,128)(2,1)S(1)}, u32[]{:S(2)}, u32[]{:S(2)}) collective-permute-start(bf16[208,512]{1,0:T(8,128)(2,1)S(1)} %fusion.1), channel_id=1, source_target_pairs={{0,48},{16,0},{32,16},{48,32},{1,49},{17,1},{33,17},{49,33},{2,50}... | collective-permute-start | bytes 638984 | tf_op jit(solution)/shard_map/ppermute | solution.py:21
  34.2 6.7 %collective-permute-done.3 = bf16[208,512]{1,0:T(8,128)(2,1)S(1)} collective-permute-done((bf16[208,512]{1,0:T(8,128)(2,1)S(1)}, bf16[208,512]{1,0:T(8,128)(2,1)S(1)}, u32[]{:S(2)}, u32[]{:S(2)}) %collective-permute-start.3) | collective-permute-done | bytes 213024 | tf_op jit(solution)/shard_map/ppermute | solution.py:21
  41.0 2.7 %collective-permute-start.16 = (bf16[4,192,512]{2,1,0:T(8,128)(2,1)S(1)}, bf16[4,192,512]{2,1,0:T(8,128)(2,1)}, u32[]{:S(2)}, u32[]{:S(2)}) collective-permute-start(bf16[4,192,512]{2,1,0:T(8,128)(2,1)S(1)} %bitcast.78), channel_id=1, source_target_pairs={{0,48},{16,0},{32,16},{48,32},{1,49},{17,1},{33,17},{49,33},{2,50}... | collective-permute-start | bytes 2359304 | tf_op jit(solution)/shard_map/ppermute | solution.py:21
  43.8 1.0 collective-permute-start.15
  44.8 0.6 pad_add_fusion.ids_ref
  45.4 0.6 pad_add_fusion.2.ids_ref
  46.0 0.7 copy.43
  46.7 0.6 collective-permute-start.13
  47.3 30.0 %collective-permute-done.16.b3 = bf16[4,192,512]{2,1,0:T(8,128)(2,1)} collective-permute-done((bf16[4,192,512]{2,1,0:T(8,128)(2,1)S(1)}, bf16[4,192,512]{2,1,0:T(8,128)(2,1)}, u32[]{:S(2)}, u32[]{:S(2)}) %collective-permute-start.16) | collective-permute-done | bytes 786464 | tf_op jit(solution)/shard_map/ppermute | solution.py:21
  77.3 3.8 %collective-permute-done.14.b1 = bf16[4,192,512]{2,1,0:T(8,128)(2,1)} collective-permute-done((bf16[4,192,512]{2,1,0:T(8,128)(2,1)S(1)}, bf16[4,192,512]{2,1,0:T(8,128)(2,1)}, u32[]{:S(2)}, u32[]{:S(2)}) %collective-permute-start.14) | collective-permute-done | bytes 786464 | tf_op jit(solution)/shard_map/ppermute | solution.py:21
  81.1 0.6 broadcast_in_dim.87.vec_ref
  81.7 14.5 %shard_map.104 = (f32[384,1002]{1,0:T(8,128)}, f32[384,1002]{1,0:T(8,128)}, f32[8,384]{1,0:T(8,128)}) custom-call(s32[3]{0:T(128)} %pad_add_fusion.2.ids_ref, f32[8,384]{1,0:T(8,128)} %broadcast_in_dim.87.vec_ref, bf16[4,192,512]{2,1,0:T(8,128)(2,1)} %bitcast.81, bf16[4,192,512]{2,1,0:T(8,128)(2,1)} %collective-permute-done.14.b1, ...), custom_call_target="tpu_custom_call" | custom-call | flops 6304038912 | bytes 19562496 | tf_op jit(solution)/shard_map/pallas_call | solution.py:128
  96.3 0.8 copy-done.3
  97.3 0.6 scatter.4.vec_ref
  97.9 15.6 %shard_map.103 = (f32[384,1002]{1,0:T(8,128)}, f32[384,1002]{1,0:T(8,128)}, f32[8,384]{1,0:T(8,128)}, bf16[384,4096]{1,0:T(8,128)(2,1)}) custom-call(s32[3]{0:T(128)} %pad_add_fusion.ids_ref, f32[8,384]{1,0:T(8,128)} %scatter.4.vec_ref, bf16[4,208,512]{2,1,0:T(8,128)(2,1)} %copy-done, bf16[4,208,512]{2,1,0:T(8,128)(2,1)} %collective-permute-done.12.b1, ...), custom_call_target="tpu_custom_call" | custom-call | flops 6304038912 | bytes 19562496 | tf_op jit(solution)/shard_map/pallas_call | solution.py:128
  113.6 0.7 add.194
  114.3 0.9 broadcast_in_dim.88
  115.2 5.8 %all-to-all-start = ((f32[64,8,384]{2,1,0:T(8,128)}), f32[64,8,384]{2,1,0:T(8,128)S(1)}, u32[]{:S(2)}, u32[]{:S(2)}) async-start(f32[64,8,384]{2,1,0:T(8,128)} %broadcast_in_dim.88), calls=%async_computation | async-start | bytes 1572864 | tf_op jit(solution)/shard_map/all_to_all | solution.py:263
  121.6 13.9 %all-to-all-done = f32[64,8,384]{2,1,0:T(8,128)S(1)} async-done(((f32[64,8,384]{2,1,0:T(8,128)}), f32[64,8,384]{2,1,0:T(8,128)S(1)}, u32[]{:S(2)}, u32[]{:S(2)}) %all-to-all-start) | async-done | bytes 786464 | tf_op jit(solution)/shard_map/all_to_all | solution.py:263
  135.4 0.4 fusion.51
  136.0 0.8 subtract_select_fusion
  136.8 0.6 concatenate.35.vec_ref
  137.4 14.5 %shard_map.105 = (bf16[1002,384]{1,0:T(8,128)(2,1)}, bf16[1002,384]{1,0:T(8,128)(2,1)}, bf16[8,8,48,512]{3,2,1,0:T(8,128)(2,1)}) custom-call(s32[3]{0:T(128)} %pad_add_fusion.ids_ref, f32[8,384]{1,0:T(8,128)} %concatenate.35.vec_ref, f32[384,1002]{1,0:T(8,128)} %get-tuple-element.37.le_own, f32[384,1002]{1,0:T(8,128)} %get-tuple-element.38.le_sib, ...), custom_call_target="tpu_custom_call" | custom-call | flops 6304038912 | bytes 19562496 | tf_op jit(solution)/shard_map/pallas_call | solution.py:174
  151.9 5.9 %all-to-all-start.1 = ((bf16[64,48,512]{2,1,0:T(8,128)(2,1)}), bf16[64,48,512]{2,1,0:T(8,128)(2,1)S(1)}, u32[]{:S(2)}, u32[]{:S(2)}) async-start(bf16[64,48,512]{2,1,0:T(8,128)(2,1)} %bitcast.75), calls=%async_computation.1 | async-start | bytes 6291456 | tf_op jit(solution)/shard_map/all_to_all | solution.py:294
  157.8 0.3 collective-permute-start.17
  158.5 0.2 fusion.11
  158.7 0.5 collective-permute-start.19
  159.2 1.1 collective-permute-done.19
  160.4 0.5 fusion.46
  160.9 12.5 %shard_map.106 = bf16[1002,4096]{1,0:T(8,128)(2,1)} custom-call(bf16[1002,384]{1,0:T(8,128)(2,1)} %get-tuple-element.42.grad_a, bf16[1002,384]{1,0:T(8,128)(2,1)} %collective-permute-done.17.grad_b, bf16[384,4096]{1,0:T(8,128)(2,1)} %get-tuple-element.44.hidden_a, bf16[384,4096]{1,0:T(8,128)(2,1)} %collective-permute-done.18.hidden_b), custom_call_target="tpu_custom_call" | custom-call | flops 6304038912 | bytes 14499840 | tf_op jit(solution)/shard_map/pallas_call | solution.py:202
  173.4 23.0 %all-to-all-done.1 = bf16[64,48,512]{2,1,0:T(8,128)(2,1)S(1)} async-done(((bf16[64,48,512]{2,1,0:T(8,128)(2,1)}), bf16[64,48,512]{2,1,0:T(8,128)(2,1)S(1)}, u32[]{:S(2)}, u32[]{:S(2)}) %all-to-all-start.1) | async-done | bytes 3145760 | tf_op jit(solution)/shard_map/all_to_all | solution.py:294
  196.4 1.1 reduce_sum.53
  (67 shorter events, 1.9 us)
Async XLA Ops:
  0.6 40.4 %collective-permute-start.9 = (bf16[1002,4096]{1,0:T(8,128)(2,1)}, bf16[1002,4096]{1,0:T(8,128)(2,1)}, u32[]{:S(2)}, u32[]{:S(2)}) collective-permute-start(bf16[1002,4096]{1,0:T(8,128)(2,1)} %bitcast.90), channel_id=1, source_target_pairs={{0,8},{8,0},{1,9},{9,1},{2,10},{10,2},{3,11},{11,3},{4,12},{12,4},... | collective-permute-start | bytes 24625160 | tf_op jit(solution)/shard_map/ppermute | solution.py:25
  0.7 40.3 %collective-permute-start.10 = (bf16[1002,4096]{1,0:T(8,128)(2,1)}, bf16[1002,4096]{1,0:T(8,128)(2,1)}, u32[]{:S(2)}, u32[]{:S(2)}) collective-permute-start(bf16[1002,4096]{1,0:T(8,128)(2,1)} %bitcast.88), channel_id=1, source_target_pairs={{0,8},{8,0},{1,9},{9,1},{2,10},{10,2},{3,11},{11,3},{4,12},{12,4},... | collective-permute-start | bytes 24625160 | tf_op jit(solution)/shard_map/ppermute | solution.py:25
  2.1 10.9 %collective-permute-start.1 = (bf16[2,48,512]{2,1,0:T(8,128)(2,1)S(1)}, bf16[2,48,512]{2,1,0:T(8,128)(2,1)S(1)}, u32[]{:S(2)}, u32[]{:S(2)}) collective-permute-start(bf16[2,48,512]{2,1,0:T(8,128)(2,1)S(1)} %pad_maximum_fusion), channel_id=1, source_target_pairs={{0,4},{2,6},{4,0},{6,2},{1,5},{3,7},{5,1},{7,3},{8,12},{10,14},{12... | collective-permute-start | bytes 294920 | tf_op jit(solution)/shard_map/ppermute | solution.py:21
  6.1 6.9 %collective-permute-start = (bf16[2,48,512]{2,1,0:T(8,128)(2,1)S(1)}, bf16[2,48,512]{2,1,0:T(8,128)(2,1)S(1)}, u32[]{:S(2)}, u32[]{:S(2)}) collective-permute-start(bf16[2,48,512]{2,1,0:T(8,128)(2,1)S(1)} %pad_maximum_fusion), channel_id=1, source_target_pairs={{0,2},{2,4},{4,6},{6,0},{1,3},{3,5},{5,7},{7,1},{8,10},{10,12},{12... | collective-permute-start | bytes 294920 | tf_op jit(solution)/shard_map/ppermute | solution.py:21
  7.1 5.9 %collective-permute-start.2 = (bf16[2,48,512]{2,1,0:T(8,128)(2,1)S(1)}, bf16[2,48,512]{2,1,0:T(8,128)(2,1)S(1)}, u32[]{:S(2)}, u32[]{:S(2)}) collective-permute-start(bf16[2,48,512]{2,1,0:T(8,128)(2,1)S(1)} %pad_maximum_fusion), channel_id=1, source_target_pairs={{0,6},{2,0},{4,2},{6,4},{1,7},{3,1},{5,3},{7,5},{8,14},{10,8},{12,... | collective-permute-start | bytes 294920 | tf_op jit(solution)/shard_map/ppermute | solution.py:21
  13.1 18.3 %collective-permute-start.8 = (bf16[4,48,512]{2,1,0:T(8,128)(2,1)S(1)}, bf16[4,48,512]{2,1,0:T(8,128)(2,1)S(1)}, u32[]{:S(2)}, u32[]{:S(2)}) collective-permute-start(bf16[4,48,512]{2,1,0:T(8,128)(2,1)S(1)} %get-tuple-element.57), channel_id=1, source_target_pairs={{0,65},{1,0},{64,1},{65,64},{2,67},{3,2},{66,3},{67,66},{4,69},{5,... | collective-permute-start | bytes 589832 | tf_op jit(solution)/shard_map/ppermute | solution.py:21
  16.2 14.5 %collective-permute-start.7 = (bf16[4,48,512]{2,1,0:T(8,128)(2,1)S(1)}, bf16[4,48,512]{2,1,0:T(8,128)(2,1)S(1)}, u32[]{:S(2)}, u32[]{:S(2)}) collective-permute-start(bf16[4,48,512]{2,1,0:T(8,128)(2,1)S(1)} %get-tuple-element.57), channel_id=1, source_target_pairs={{0,64},{1,65},{64,0},{65,1},{2,66},{3,67},{66,2},{67,3},{4,68},{5,... | collective-permute-start | bytes 589832 | tf_op jit(solution)/shard_map/ppermute | solution.py:21
  16.8 10.9 %collective-permute-start.6 = (bf16[4,48,512]{2,1,0:T(8,128)(2,1)S(1)}, bf16[4,48,512]{2,1,0:T(8,128)(2,1)S(1)}, u32[]{:S(2)}, u32[]{:S(2)}) collective-permute-start(bf16[4,48,512]{2,1,0:T(8,128)(2,1)S(1)} %get-tuple-element.57), channel_id=1, source_target_pairs={{0,1},{1,64},{64,65},{65,0},{2,3},{3,66},{66,67},{67,2},{4,5},{5,6... | collective-permute-start | bytes 589832 | tf_op jit(solution)/shard_map/ppermute | solution.py:21
  27.7 13.3 %collective-permute-start.4 = (bf16[208,512]{1,0:T(8,128)(2,1)S(1)}, bf16[208,512]{1,0:T(8,128)(2,1)S(1)}, u32[]{:S(2)}, u32[]{:S(2)}) collective-permute-start(bf16[208,512]{1,0:T(8,128)(2,1)S(1)} %fusion.1), channel_id=1, source_target_pairs={{0,32},{16,48},{32,0},{48,16},{1,33},{17,49},{33,1},{49,17},{2,34}... | collective-permute-start | bytes 638984 | tf_op jit(solution)/shard_map/ppermute | solution.py:21
  30.7 10.2 %collective-permute-start.3 = (bf16[208,512]{1,0:T(8,128)(2,1)S(1)}, bf16[208,512]{1,0:T(8,128)(2,1)S(1)}, u32[]{:S(2)}, u32[]{:S(2)}) collective-permute-start(bf16[208,512]{1,0:T(8,128)(2,1)S(1)} %fusion.1), channel_id=1, source_target_pairs={{0,16},{16,32},{32,48},{48,0},{1,17},{17,33},{33,49},{49,1},{2,18}... | collective-permute-start | bytes 638984 | tf_op jit(solution)/shard_map/ppermute | solution.py:21
  31.4 9.6 %collective-permute-start.5 = (bf16[208,512]{1,0:T(8,128)(2,1)S(1)}, bf16[208,512]{1,0:T(8,128)(2,1)S(1)}, u32[]{:S(2)}, u32[]{:S(2)}) collective-permute-start(bf16[208,512]{1,0:T(8,128)(2,1)S(1)} %fusion.1), channel_id=1, source_target_pairs={{0,48},{16,0},{32,16},{48,32},{1,49},{17,1},{33,17},{49,33},{2,50}... | collective-permute-start | bytes 638984 | tf_op jit(solution)/shard_map/ppermute | solution.py:21
  34.2 47.5 %copy-start.1 = (bf16[4,4,48,512]{3,2,1,0:T(8,128)(2,1)}, bf16[4,4,48,512]{3,2,1,0:T(8,128)(2,1)S(1)}, u32[]{:S(2)}) copy-start(bf16[4,4,48,512]{3,2,1,0:T(8,128)(2,1)S(1)} %bitcast_dynamic-update-slice_fusion.4) | copy-start | bytes 2359300
  41.0 55.2 %copy-start = (bf16[4,208,512]{2,1,0:T(8,128)(2,1)}, bf16[4,208,512]{2,1,0:T(8,128)(2,1)S(1)}, u32[]{:S(2)}) copy-start(bf16[4,208,512]{2,1,0:T(8,128)(2,1)S(1)} %bitcast_dynamic-update-slice_fusion.b0) | copy-start | bytes 2555908
  41.0 36.3 %collective-permute-start.16 = (bf16[4,192,512]{2,1,0:T(8,128)(2,1)S(1)}, bf16[4,192,512]{2,1,0:T(8,128)(2,1)}, u32[]{:S(2)}, u32[]{:S(2)}) collective-permute-start(bf16[4,192,512]{2,1,0:T(8,128)(2,1)S(1)} %bitcast.78), channel_id=1, source_target_pairs={{0,48},{16,0},{32,16},{48,32},{1,49},{17,1},{33,17},{49,33},{2,50}... | collective-permute-start | bytes 2359304 | tf_op jit(solution)/shard_map/ppermute | solution.py:21
  43.8 33.5 %collective-permute-start.15 = (bf16[4,192,512]{2,1,0:T(8,128)(2,1)S(1)}, bf16[4,192,512]{2,1,0:T(8,128)(2,1)}, u32[]{:S(2)}, u32[]{:S(2)}) collective-permute-start(bf16[4,192,512]{2,1,0:T(8,128)(2,1)S(1)} %bitcast.79), channel_id=1, source_target_pairs={{0,32},{16,48},{32,0},{48,16},{1,33},{17,49},{33,1},{49,17},{2,34}... | collective-permute-start | bytes 2359304 | tf_op jit(solution)/shard_map/ppermute | solution.py:21
  44.7 36.3 %collective-permute-start.14 = (bf16[4,192,512]{2,1,0:T(8,128)(2,1)S(1)}, bf16[4,192,512]{2,1,0:T(8,128)(2,1)}, u32[]{:S(2)}, u32[]{:S(2)}) collective-permute-start(bf16[4,192,512]{2,1,0:T(8,128)(2,1)S(1)} %bitcast.80), channel_id=1, source_target_pairs={{0,16},{16,32},{32,48},{48,0},{1,17},{17,33},{33,49},{49,1},{2,18}... | collective-permute-start | bytes 2359304 | tf_op jit(solution)/shard_map/ppermute | solution.py:21
  45.4 50.9 %collective-permute-start.11 = (bf16[4,208,512]{2,1,0:T(8,128)(2,1)S(1)}, bf16[4,208,512]{2,1,0:T(8,128)(2,1)S(1)}, u32[]{:S(2)}, u32[]{:S(2)}) collective-permute-start(bf16[4,208,512]{2,1,0:T(8,128)(2,1)S(1)} %bitcast_dynamic-update-slice_fusion.b0), channel_id=1, source_target_pairs={{0,64},{1,65},{64,0},{65,1},{2,66},{3,67},{66,2},{67,3},{4,68},{5,... | collective-permute-start | bytes 2555912 | tf_op jit(solution)/shard_map/ppermute | solution.py:21
  46.7 51.3 %collective-permute-start.13 = (bf16[4,208,512]{2,1,0:T(8,128)(2,1)S(1)}, bf16[4,208,512]{2,1,0:T(8,128)(2,1)}, u32[]{:S(2)}, u32[]{:S(2)}) collective-permute-start(bf16[4,208,512]{2,1,0:T(8,128)(2,1)S(1)} %bitcast_dynamic-update-slice_fusion.b0), channel_id=1, source_target_pairs={{0,65},{1,0},{64,1},{65,64},{2,67},{3,2},{66,3},{67,66},{4,69},{5,... | collective-permute-start | bytes 2555912 | tf_op jit(solution)/shard_map/ppermute | solution.py:21
  77.3 20.6 %collective-permute-start.12 = (bf16[4,208,512]{2,1,0:T(8,128)(2,1)S(1)}, bf16[4,208,512]{2,1,0:T(8,128)(2,1)}, u32[]{:S(2)}, u32[]{:S(2)}) collective-permute-start(bf16[4,208,512]{2,1,0:T(8,128)(2,1)S(1)} %bitcast_dynamic-update-slice_fusion.b0), channel_id=1, source_target_pairs={{0,1},{1,64},{64,65},{65,0},{2,3},{3,66},{66,67},{67,2},{4,5},{5,6... | collective-permute-start | bytes 2555912 | tf_op jit(solution)/shard_map/ppermute | solution.py:21
  96.2 0.9 copy-start.3
  97.9 15.6 %copy-start.2 = (f32[8,384]{1,0:T(8,128)S(1)}, f32[8,384]{1,0:T(8,128)}, u32[]{:S(2)}) copy-start(f32[8,384]{1,0:T(8,128)} %get-tuple-element.36) | copy-start | bytes 36868
  115.2 20.2 %all-to-all-start = ((f32[64,8,384]{2,1,0:T(8,128)}), f32[64,8,384]{2,1,0:T(8,128)S(1)}, u32[]{:S(2)}, u32[]{:S(2)}) async-start(f32[64,8,384]{2,1,0:T(8,128)} %broadcast_in_dim.88), calls=%async_computation | async-start | bytes 1572864 | tf_op jit(solution)/shard_map/all_to_all | solution.py:263
  121.5 39.5 %collective-permute-start.18 = (bf16[384,4096]{1,0:T(8,128)(2,1)}, bf16[384,4096]{1,0:T(8,128)(2,1)}, u32[]{:S(2)}, u32[]{:S(2)}) collective-permute-start(bf16[384,4096]{1,0:T(8,128)(2,1)} %get-tuple-element.44.hidden_a), channel_id=1, source_target_pairs={{0,8},{8,0},{1,9},{9,1},{2,10},{10,2},{3,11},{11,3},{4,12},{12,4},... | collective-permute-start | bytes 9437192 | tf_op jit(solution)/shard_map/ppermute | solution.py:25
  151.9 44.5 %all-to-all-start.1 = ((bf16[64,48,512]{2,1,0:T(8,128)(2,1)}), bf16[64,48,512]{2,1,0:T(8,128)(2,1)S(1)}, u32[]{:S(2)}, u32[]{:S(2)}) async-start(bf16[64,48,512]{2,1,0:T(8,128)(2,1)} %bitcast.75), calls=%async_computation.1 | async-start | bytes 6291456 | tf_op jit(solution)/shard_map/all_to_all | solution.py:294
  157.8 3.1 %collective-permute-start.17 = (bf16[1002,384]{1,0:T(8,128)(2,1)}, bf16[1002,384]{1,0:T(8,128)(2,1)}, u32[]{:S(2)}, u32[]{:S(2)}) collective-permute-start(bf16[1002,384]{1,0:T(8,128)(2,1)} %get-tuple-element.43), channel_id=1, source_target_pairs={{0,8},{8,0},{1,9},{9,1},{2,10},{10,2},{3,11},{11,3},{4,12},{12,4},... | collective-permute-start | bytes 2308616 | tf_op jit(solution)/shard_map/ppermute | solution.py:25
  158.7 1.7 collective-permute-start.19

commit v3 on v2

--- a/solution.py
+++ b/solution.py
@@ -56,23 +56,26 @@
     return [turned[:, k : k + 1] for k in range(8)]
 
 
-def place_blocks(x_ring, ids_ref, blocks, out_ref):
-    rows, feats = blocks[0].shape[-2:]
-    for by, block in enumerate(blocks):
-        place = (ids_ref[2] - by) & 3
-        if x_ring:
-            for y in range(4):
-                at = pl.multiple_of(((y // 2) * 4 + place) * rows, rows)
-                out_ref[pl.ds(at, rows), (y % 2) * feats : (y % 2 + 1) * feats] = block[y]
-        else:
-            at = pl.multiple_of((place // 2) * 4 * rows, 4 * rows)
-            lane = pl.multiple_of((place % 2) * feats, feats)
-            out_ref[pl.ds(at, 4 * rows), pl.ds(lane, feats)] = block[...].reshape(4 * rows, feats)
-
-
-def q_kernel(x_ring, ids_ref, vec_ref, b0, b1, b2, b3, own_ref, sib_ref, e_own, e_sib, stats_ref, hidden_ref):
+def place_blocks(ids_ref, y_blocks, x_blocks, x_ring, out_ref):
+    rows, half = y_blocks[0].shape[-2:]
+    feats = 2 * half
+    for by, block in enumerate(y_blocks):
+        y = (ids_ref[2] - by) & 3
+        at = pl.multiple_of((y // 2) * 4 * rows, 4 * rows)
+        lane = pl.multiple_of((y % 2) * feats, feats)
+        out_ref[pl.ds(at, 4 * rows), pl.ds(lane, half)] = block[...].reshape(4 * rows, half)
+    for by, block in enumerate(x_blocks):
+        x = (ids_ref[3] - by) & 3 if x_ring else by
+        for y in range(4):
+            at = pl.multiple_of(((y // 2) * 4 + x) * rows, rows)
+            lane = (y % 2) * feats + half
+            out_ref[pl.ds(at, rows), lane : lane + half] = block[y]
+
+
+def q_kernel(learner, ids_ref, vec_ref, *refs):
+    blocks, (own_ref, sib_ref, e_own, e_sib, stats_ref, hidden_ref) = refs[:8], refs[8:]
     j = pl.program_id(0)
-    place_blocks(x_ring, ids_ref, (b0, b1, b2, b3), hidden_ref)
+    place_blocks(ids_ref, blocks[:4], blocks[4:], learner, hidden_ref)
     for head_ref, q_ref in ((own_ref, e_own), (sib_ref, e_sib)):
         part = lax.dot_general(hidden_ref[...], head_ref[...], NT, preferred_element_type=jnp.float32)
 
@@ -91,44 +94,54 @@
         )
         total = jnp.zeros_like(peak)
         picked = jnp.zeros_like(peak)
-        if not x_ring:
+        if learner:
             action = columns_of(vec_ref)[0].astype(jnp.int32)
             ids = lax.broadcasted_iota(jnp.int32, e_own.shape, 1)
         for k, q_ref in enumerate((e_own, e_sib)):
             q = q_ref[...]
-            if not x_ring:
+            if learner:
                 hit = ids == action - ids_ref[k]
                 picked += jnp.sum(jnp.where(hit, q, 0.0), axis=1, keepdims=True)
             expo = jnp.exp((q - peak) / temper)
             total += jnp.sum(expo, axis=1, keepdims=True)
             q_ref[...] = expo
         lane = lax.broadcasted_iota(jnp.int32, (peak.shape[0], 128), 1)
-        first = 2 if x_ring else 0
+        first = 0 if learner else 2
         table = jnp.where(lane == first, peak, jnp.where(lane == first + 1, total, 0.0))
-        if not x_ring:
+        if learner:
             table = jnp.where(lane == 4, picked, table)
-        stats_ref[...] = table.T[:8]
-
-
-def q_values(blocks, heads, ids, vec, x_ring, rows):
+        table = table.T[:8]
+        if learner:
+            stats_ref[...] = table
+        else:
+            stats_ref[...] = jnp.broadcast_to(table + vec_ref[...], stats_ref.shape)
+
+
+def q_values(blocks, heads, ids, vec, learner, rows):
     width, feats_all = heads[0].shape
-    feats = blocks[0].shape[-1]
+    half = blocks[0].shape[-1]
+    feats = 2 * half
     tokens = vec.shape[1]
-    block_spec = pl.BlockSpec((4, rows, feats), lambda j: (0, j, 0))
+    block_specs = [pl.BlockSpec((4, rows, half), lambda j: (0, j, 0))] * len(blocks)
+    if not learner:
+        blocks = blocks[:4] + blocks[4:] * 4
+        block_specs = block_specs[:4] + [
+            pl.BlockSpec((None, 4, rows, half), lambda j, x=x: (x, 0, j, 0)) for x in range(4)
+        ]
     head_spec = pl.BlockSpec((width, 2 * feats), lambda j: (0, j))
     hidden_spec = pl.BlockSpec((tokens, 2 * feats), lambda j: (0, j))
     q_shape = jax.ShapeDtypeStruct((tokens, width), jnp.float32)
-    stats_shape = jax.ShapeDtypeStruct((8, tokens), jnp.float32)
+    stats_shape = jax.ShapeDtypeStruct((8, tokens) if learner else (64, 8, tokens), jnp.float32)
     hidden_shape = jax.ShapeDtypeStruct((tokens, feats_all), jnp.bfloat16)
     outs = [q_shape, q_shape, stats_shape]
     out_specs = [whole(o.shape) for o in outs]
     scratch = [pltpu.VMEM((tokens, 2 * feats), jnp.bfloat16)]
-    if not x_ring:
+    if learner:
         outs, out_specs, scratch = outs + [hidden_shape], out_specs + [hidden_spec], []
     return pl.pallas_call(
-        functools.partial(q_kernel, x_ring),
+        functools.partial(q_kernel, learner),
         grid=(feats_all // (2 * feats),),
-        in_specs=[pl.BlockSpec(memory_space=pltpu.SMEM), whole(vec.shape)] + [block_spec] * 4 + [head_spec] * 2,
+        in_specs=[pl.BlockSpec(memory_space=pltpu.SMEM), whole(vec.shape)] + block_specs + [head_spec] * 2,
         out_specs=out_specs,
         out_shape=outs,
         scratch_shapes=scratch,
@@ -219,24 +232,40 @@
     seq_len = rows // trajs
     traj_total = trajs * 16
 
+    half = feats // 2
+
     learn_head, target_head = learn_head.T, target_head.T
-    learn_sib, target_sib = swap_cores(learn_head), swap_cores(target_head)
+    learn_sib = swap_cores(learn_head)
 
     extra = [action & 255, (action >> 8) & 255, action >> 16, reward, traj_len, owner]
     extra = jnp.concatenate([v.astype(bf16) for v in extra])
-    extra = jnp.pad(extra[None], ((0, 15), (0, feats - extra.shape[0])))
-
-    both = gather_ring(jnp.stack([learn_hidden, target_hidden]), "z")
-    learn = gather_ring(jnp.concatenate([both[:, 0].reshape(4 * rows, feats), extra]), "x")
-    target = gather_ring(both[:, 1], Y)
-    learn, target, learn_sib, target_sib = lax.optimization_barrier(
-        (learn, target, learn_sib, target_sib)
-    )
-    learn_blocks = ring_blocks(learn, Y)
-    target_blocks = ring_blocks(target.reshape(4, 4 * rows, feats), "x")
+    extra = jnp.pad(extra[None], ((0, 15), (0, half - extra.shape[0])))
+
+    both = jnp.stack([learn_hidden, target_hidden]).reshape(2, rows, 2, half).transpose(2, 0, 1, 3)
+    both, learn_sib = lax.optimization_barrier((gather_ring(both, "z"), learn_sib))
+    block = 4 * rows
+    first, second = (
+        [both[:, part, head].reshape(block, half) for head in (0, 1)] for part in (0, 1)
+    )
+    first = gather_ring(jnp.concatenate([first[0], extra, first[1]]), "x")
+    second = gather_ring(jnp.concatenate(second), Y)
+    first, second = lax.optimization_barrier((first, second))
+    learn_y = ring_blocks(first[:, : block + 16], Y)
+    learn_x = ring_blocks(second[:, :block], "x")
+    first, second = first[:, block + 16 :], second[:, block:]
+    first, second, target_head, *near = lax.optimization_barrier(
+        (first, second, target_head, learn_y[1], learn_y[3], learn_x[1], learn_x[3])
+    )
+    target_sib = swap_cores(target_head)
+    learn_y = (learn_y[0], near[0], learn_y[2], near[1])
+    learn_x = (learn_x[0], near[2], learn_x[2], near[3])
+    target_y = ring_blocks(first, Y)
+    target_x = lax.all_to_all(
+        jnp.broadcast_to(second[None], (4,) + second.shape), "x", 0, 0, tiled=True
+    )
     learn_heads, target_heads = (learn_head, learn_sib), (target_head, target_sib)
 
-    mine, other = (learn_blocks[by][:, 4 * rows].astype(f32) for by in (0, 2))
+    mine, other = (learn_y[by][:, block].astype(f32) for by in (0, 2))
     lower = lax.axis_index("yh") == 0
     small = jnp.concatenate([jnp.where(lower, mine, other), jnp.where(lower, other, mine)])
 
@@ -252,17 +281,15 @@
     dp = lax.axis_index(DP)
     tensor = lax.axis_index(TENSOR)
     bases = [((dp + (1 - 2 * core) * k) * 8 + tensor) * width for k in (0, 1)]
-    learn_ids = jnp.stack(bases + [lax.axis_index(Y)])
-    target_ids = jnp.stack(bases + [lax.axis_index("x")])
-
-    zeros = jnp.zeros((8, tokens), f32)
-    *learn_e, learn_stats, learn = q_values(learn_blocks, learn_heads, learn_ids, zeros.at[0].set(action_all), False, rows)
-    *target_e, target_stats = q_values(target_blocks, target_heads, target_ids, zeros, True, rows)
-
-    packed = learn_stats + target_stats
-    packed = lax.all_to_all(
-        jnp.broadcast_to(packed[None], (64,) + packed.shape), PLANE, 0, 0, tiled=True
-    )
+    ids = jnp.stack(bases + [lax.axis_index(Y), lax.axis_index("x")])
+
+    vec = jnp.zeros((8, tokens), f32).at[0].set(action_all)
+    *learn_e, learn_stats, learn = q_values(
+        learn_y + learn_x, learn_heads, ids, vec, True, rows
+    )
+    *target_e, target_stats = q_values(target_y + (target_x,), target_heads, ids, learn_stats, False, rows)
+
+    packed = lax.all_to_all(target_stats, PLANE, 0, 0, tiled=True)
     learn_max = jnp.max(packed[:, 0], axis=0)
     target_max = jnp.max(packed[:, 2], axis=0)
     learn_sum = jnp.sum(packed[:, 1] * jnp.exp((packed[:, 0] - learn_max) / temper), axis=0)
@@ -282,13 +309,13 @@
         [
             action_all,
             kl_weight * live * jnp.exp((learn_stats[0] - learn_max) / temper) / learn_sum,
-            kl_weight * live * jnp.exp((target_stats[2] - target_max) / temper) / target_sum,
+            kl_weight * live * jnp.exp((target_stats[0, 2] - target_max) / temper) / target_sum,
             delta,
         ]
     )
     vec = jnp.concatenate([vec, jnp.zeros_like(vec)])
     grad_own, grad_sib, partial = gradients(
-        learn_e, target_e, learn_heads, learn_ids, vec, rows, feats, traj_total
+        learn_e, target_e, learn_heads, ids, vec, rows, feats, traj_total
     )
 
     partial = lax.all_to_all(partial.reshape(64, rows, feats), PLANE, 0, 0, tiled=True)

time: 198 us -> 184 us (0.929)
  waiting for transfers between devices: 88.2 us -> 58.6 us
  starting transfers between devices: 36 us -> 49.7 us
  local copies, waits for them, and re-layouts: 6.24 us -> 8.93 us
    ppermute x15 -> x18, waiting for transfers between devices: 50.2 us -> 19.5 us  [shift(): return lax.ppermute(v, axis, [(i, (i + by) % 4) for i in range(4)])]
    ppermute x15 -> x18, starting transfers between devices: 22.8 us -> 30.5 us  [shift(): return lax.ppermute(v, axis, [(i, (i + by) % 4) for i in range(4)])]
    all_to_all x1 -> x2, starting transfers between devices: 5.83 us -> 12.3 us  [the longest x1 8.73 us: shards(): packed = lax.all_to_all(target_stats, PLANE, 0, 0, tiled=True)]
    all_to_all x1 -> x2, waiting for transfers between devices: 13.9 us -> 14.1 us  [the longest x1 14.1 us: shards(): packed = lax.all_to_all(target_stats, PLANE, 0, 0, tiled=True)]
  transfers between devices with their start and end apart: 22 -> 26, of which waited for: 7 -> 11; matrix products, arithmetic and copies ran while one was open for 6% -> 7% of each run, Pallas kernels for 21% -> 23%
where the time goes in v3:
time: 184 us; the launch traced here: 183 us
  waiting for transfers between devices  58.6 us (32%)
  Pallas kernels  57.5 us (31%)
  starting transfers between devices  49.7 us (27%)
  local copies, waits for them, and re-layouts  8.93 us (5%)
  other arithmetic  7.29 us (4%)
    ppermute x18, starting transfers between devices, shift(): return lax.ppermute(v, axis, [(i, (i + by) % 4) for i in range(4)])  30.5 us
    pallas_call x2, Pallas kernels, q_values(): pl.pallas_call(functools.partial(q_kernel, learner), grid=(feats_all // (...  30.5 us
    all_to_all x1, waiting for transfers between devices, shards(): lax.all_to_all(partial.reshape(64, rows, feats), PLANE, 0, 0, tiled=True)  23.1 us
    ppermute x18, waiting for transfers between devices, shift(): return lax.ppermute(v, axis, [(i, (i + by) % 4) for i in range(4)])  19.5 us
    pallas_call x1, Pallas kernels, gradients(): pl.pallas_call(functools.partial(grad_kernel, 1.0 / traj_total), grid=(fe...  14.5 us
    all_to_all x1, waiting for transfers between devices, shards(): packed = lax.all_to_all(target_stats, PLANE, 0, 0, tiled=True)  14.1 us
    pallas_call x1, Pallas kernels, head_gradient(): pl.pallas_call(head_kernel, grid=(4,), in_specs=[whole((width, tokens))]...  12.5 us
    all_to_all x1, starting transfers between devices, shards(): packed = lax.all_to_all(target_stats, PLANE, 0, 0, tiled=True)  8.73 us
  transfers between devices with their start and end apart: 26, of which 11 were waited for; matrix products, arithmetic and copies ran while one was open for 7% of the time, Pallas kernels for 23%

profile of v3, /device:TPU:0, one launch (start us, length us, event | category | flops | bytes accessed | tf_op | source)
XLA Modules:
  0.0 183.2 jit_solution(16198924773746787242)
XLA Ops:
  0.7 0.8 stack.33
  1.5 0.8 stack.34
  2.4 2.1 %collective-permute-start = (bf16[2,2,48,256]{3,2,1,0:T(8,128)(2,1)S(1)}, bf16[2,2,48,256]{3,2,1,0:T(8,128)(2,1)S(1)}, u32[]{:S(2)}, u32[]{:S(2)}) collective-permute-start(bf16[2,2,48,256]{3,2,1,0:T(8,128)(2,1)S(1)} %bitcast.90), channel_id=1, source_target_pairs={{0,2},{2,4},{4,6},{6,0},{1,3},{3,5},{5,7},{7,1},{8,10},{10,12},{12... | collective-permute-start | bytes 294920 | tf_op jit(solution)/shard_map/ppermute | solution.py:21
  4.5 3.6 %collective-permute-start.1 = (bf16[2,2,48,256]{3,2,1,0:T(8,128)(2,1)S(1)}, bf16[2,2,48,256]{3,2,1,0:T(8,128)(2,1)S(1)}, u32[]{:S(2)}, u32[]{:S(2)}) collective-permute-start(bf16[2,2,48,256]{3,2,1,0:T(8,128)(2,1)S(1)} %bitcast.91), channel_id=1, source_target_pairs={{0,4},{2,6},{4,0},{6,2},{1,5},{3,7},{5,1},{7,3},{8,12},{10,14},{12... | collective-permute-start | bytes 294920 | tf_op jit(solution)/shard_map/ppermute | solution.py:21
  8.0 1.0 collective-permute-start.2
  9.1 0.7 shift-right-arithmetic_convert_fusion
  9.8 0.7 convert_element_type.49
  10.4 0.7 convert_element_type.50
  11.1 0.8 concatenate.34
  11.9 1.4 collective-permute-done.1
  13.4 0.7 collective-permute-done.3.refs_9_.sib_ref
  14.1 1.7 collective-permute-start.7
  15.8 2.9 %collective-permute-start.8 = (bf16[384,256]{1,0:T(8,128)(2,1)S(1)}, bf16[384,256]{1,0:T(8,128)(2,1)S(1)}, u32[]{:S(2)}, u32[]{:S(2)}) collective-permute-start(bf16[384,256]{1,0:T(8,128)(2,1)S(1)} %pad_maximum_fusion), channel_id=1, source_target_pairs={{0,64},{1,65},{64,0},{65,1},{2,66},{3,67},{66,2},{67,3},{4,68},{5,... | collective-permute-start | bytes 589832 | tf_op jit(solution)/shard_map/ppermute | solution.py:21
  18.7 1.3 collective-permute-start.9
  20.1 1.6 collective-permute-start.4
  21.6 2.7 %collective-permute-start.5 = (bf16[400,256]{1,0:T(8,128)(2,1)S(1)}, bf16[400,256]{1,0:T(8,128)(2,1)S(1)}, u32[]{:S(2)}, u32[]{:S(2)}) collective-permute-start(bf16[400,256]{1,0:T(8,128)(2,1)S(1)} %fusion.3), channel_id=1, source_target_pairs={{0,32},{16,48},{32,0},{48,16},{1,33},{17,49},{33,1},{49,17},{2,34}... | collective-permute-start | bytes 614408 | tf_op jit(solution)/shard_map/ppermute | solution.py:21
  24.6 1.5 collective-permute-start.6
  26.1 1.8 collective-permute-done.8
  28.4 4.6 %collective-permute-done.5 = bf16[400,256]{1,0:T(8,128)(2,1)S(1)} collective-permute-done((bf16[400,256]{1,0:T(8,128)(2,1)S(1)}, bf16[400,256]{1,0:T(8,128)(2,1)S(1)}, u32[]{:S(2)}, u32[]{:S(2)}) %collective-permute-start.5) | collective-permute-done | bytes 204832 | tf_op jit(solution)/shard_map/ppermute | solution.py:21
  33.1 0.7 collective-permute-start.11
  33.9 2.6 %collective-permute-start.12 = (bf16[4,208,256]{2,1,0:T(8,128)(2,1)S(1)}, bf16[4,208,256]{2,1,0:T(8,128)(2,1)S(1)}, u32[]{:S(2)}, u32[]{:S(2)}) collective-permute-start(bf16[4,208,256]{2,1,0:T(8,128)(2,1)S(1)} %slice.94.refs_0_), channel_id=1, source_target_pairs={{0,65},{1,0},{64,1},{65,64},{2,67},{3,2},{66,3},{67,66},{4,69},{5,... | collective-permute-start | bytes 1277960 | tf_op jit(solution)/shard_map/ppermute | solution.py:21
  36.5 1.7 collective-permute-start.13
  38.2 1.6 collective-permute-start.14
  39.8 6.8 %collective-permute-done.13.refs_5_ = bf16[4,192,256]{2,1,0:T(8,128)(2,1)S(1)} collective-permute-done((bf16[4,192,256]{2,1,0:T(8,128)(2,1)S(1)}, bf16[4,192,256]{2,1,0:T(8,128)(2,1)S(1)}, u32[]{:S(2)}, u32[]{:S(2)}) %collective-permute-start.13) | collective-permute-done | bytes 393248 | tf_op jit(solution)/shard_map/ppermute | solution.py:21
  46.6 1.4 collective-permute-done.14.refs_7_
  48.0 0.9 copy-done.6
  49.1 0.7 pad_add_fusion.ids_ref
  50.1 1.9 %collective-permute-start.15 = (bf16[4,192,256]{2,1,0:T(8,128)(2,1)}, bf16[4,192,256]{2,1,0:T(8,128)(2,1)}, u32[]{:S(2)}, u32[]{:S(2)}) collective-permute-start(bf16[4,192,256]{2,1,0:T(8,128)(2,1)} %copy-done.3), channel_id=1, source_target_pairs={{0,32},{16,48},{32,0},{48,16},{1,33},{17,49},{33,1},{49,17},{2,34}... | collective-permute-start | bytes 1179656 | tf_op jit(solution)/shard_map/ppermute | solution.py:21
  52.0 0.9 collective-permute-start.16
  52.9 2.3 %collective-permute-start.17 = (bf16[4,192,256]{2,1,0:T(8,128)(2,1)S(1)}, bf16[4,192,256]{2,1,0:T(8,128)(2,1)}, u32[]{:S(2)}, u32[]{:S(2)}) collective-permute-start(bf16[4,192,256]{2,1,0:T(8,128)(2,1)S(1)} %slice.100.refs_0_), channel_id=1, source_target_pairs={{0,64},{1,65},{64,0},{65,1},{2,66},{3,67},{66,2},{67,3},{4,68},{5,... | collective-permute-start | bytes 1179656 | tf_op jit(solution)/shard_map/ppermute | solution.py:21
  55.3 1.4 broadcast_in_dim.85
  56.6 3.6 %all-to-all-start = ((bf16[4,4,192,256]{3,2,1,0:T(8,128)(2,1)}), bf16[4,4,192,256]{3,2,1,0:T(8,128)(2,1)S(1)}, u32[]{:S(2)}, u32[]{:S(2)}) async-start(bf16[4,4,192,256]{3,2,1,0:T(8,128)(2,1)} %broadcast_in_dim.85), calls=%async_computation | async-start | bytes 3145728 | tf_op jit(solution)/shard_map/all_to_all | solution.py:263
  60.2 3.1 %collective-permute-done.10.refs_2_ = bf16[4,208,256]{2,1,0:T(8,128)(2,1)} collective-permute-done((bf16[4,208,256]{2,1,0:T(8,128)(2,1)S(1)}, bf16[4,208,256]{2,1,0:T(8,128)(2,1)}, u32[]{:S(2)}, u32[]{:S(2)}) %collective-permute-start.10) | collective-permute-done | bytes 426016 | tf_op jit(solution)/shard_map/ppermute | solution.py:21
  63.5 0.7 broadcast_select_fusion
  64.3 0.7 slice_convert_fusion
  65.8 15.6 %shard_map.103 = (f32[384,1002]{1,0:T(8,128)}, f32[384,1002]{1,0:T(8,128)}, f32[8,384]{1,0:T(8,128)}, bf16[384,4096]{1,0:T(8,128)(2,1)}) custom-call(s32[4]{0:T(128)} %pad_add_fusion.ids_ref, f32[8,384]{1,0:T(8,128)} %scatter.4.vec_ref, bf16[4,208,256]{2,1,0:T(8,128)(2,1)} %copy-done.2, bf16[4,208,256]{2,1,0:T(8,128)(2,1)} %copy-done.5, ...), custom_call_target="tpu_custom_call" | custom-call | flops 6304038912 | bytes 19562496 | tf_op jit(solution)/shard_map/pallas_call | solution.py:141
  81.5 0.7 copy-done.4
  82.8 14.8 %shard_map.104 = (f32[384,1002]{1,0:T(8,128)}, f32[384,1002]{1,0:T(8,128)}, f32[64,8,384]{2,1,0:T(8,128)}) custom-call(s32[4]{0:T(128)} %pad_add_fusion.ids_ref, f32[8,384]{1,0:T(8,128)} %get-tuple-element.46.vec_ref, bf16[4,192,256]{2,1,0:T(8,128)(2,1)} %copy-done.1, bf16[4,192,256]{2,1,0:T(8,128)(2,1)} %collective-permute-done.16.refs_1_, ...), custom_call_target="tpu_custom_call" | custom-call | flops 6304038912 | bytes 19562496 | tf_op jit(solution)/shard_map/pallas_call | solution.py:141
  97.6 8.7 %all-to-all-start.1 = ((f32[64,8,384]{2,1,0:T(8,128)}), f32[64,8,384]{2,1,0:T(8,128)S(1)}, u32[]{:S(2)}, u32[]{:S(2)}) async-start(f32[64,8,384]{2,1,0:T(8,128)} %get-tuple-element.50), calls=%async_computation.1 | async-start | bytes 1572864 | tf_op jit(solution)/shard_map/all_to_all | solution.py:292
  106.9 14.1 %all-to-all-done.1 = f32[64,8,384]{2,1,0:T(8,128)S(1)} async-done(((f32[64,8,384]{2,1,0:T(8,128)}), f32[64,8,384]{2,1,0:T(8,128)S(1)}, u32[]{:S(2)}, u32[]{:S(2)}) %all-to-all-start.1) | async-done | bytes 786464 | tf_op jit(solution)/shard_map/all_to_all | solution.py:292
  121.5 0.8 subtract_select_fusion
  122.3 0.6 concatenate.40.vec_ref
  123.0 14.5 %shard_map.105 = (bf16[1002,384]{1,0:T(8,128)(2,1)}, bf16[1002,384]{1,0:T(8,128)(2,1)}, bf16[8,8,48,512]{3,2,1,0:T(8,128)(2,1)}) custom-call(s32[4]{0:T(128)} %pad_add_fusion.ids_ref, f32[8,384]{1,0:T(8,128)} %concatenate.40.vec_ref, f32[384,1002]{1,0:T(8,128)} %get-tuple-element.51.le_own, f32[384,1002]{1,0:T(8,128)} %get-tuple-element.52.le_sib, ...), custom_call_target="tpu_custom_call" | custom-call | flops 6304038912 | bytes 19562496 | tf_op jit(solution)/shard_map/pallas_call | solution.py:187
  137.5 5.9 %all-to-all-start.2 = ((bf16[64,48,512]{2,1,0:T(8,128)(2,1)}), bf16[64,48,512]{2,1,0:T(8,128)(2,1)S(1)}, u32[]{:S(2)}, u32[]{:S(2)}) async-start(bf16[64,48,512]{2,1,0:T(8,128)(2,1)} %bitcast.81), calls=%async_computation.2 | async-start | bytes 6291456 | tf_op jit(solution)/shard_map/all_to_all | solution.py:321
  144.8 1.1 collective-permute-done.22
  146.5 12.5 %shard_map.106 = bf16[1002,4096]{1,0:T(8,128)(2,1)} custom-call(bf16[1002,384]{1,0:T(8,128)(2,1)} %get-tuple-element.56.grad_a, bf16[1002,384]{1,0:T(8,128)(2,1)} %collective-permute-done.20.grad_b, bf16[384,4096]{1,0:T(8,128)(2,1)} %get-tuple-element.58.hidden_a, bf16[384,4096]{1,0:T(8,128)(2,1)} %collective-permute-done.21.hidden_b), custom_call_target="tpu_custom_call" | custom-call | flops 6304038912 | bytes 14499840 | tf_op jit(solution)/shard_map/pallas_call | solution.py:215
  159.0 23.1 %all-to-all-done.2 = bf16[64,48,512]{2,1,0:T(8,128)(2,1)S(1)} async-done(((bf16[64,48,512]{2,1,0:T(8,128)(2,1)}), bf16[64,48,512]{2,1,0:T(8,128)(2,1)S(1)}, u32[]{:S(2)}, u32[]{:S(2)}) %all-to-all-start.2) | async-done | bytes 3145760 | tf_op jit(solution)/shard_map/all_to_all | solution.py:321
  182.1 1.1 reduce_sum.53
  (89 shorter events, 6.3 us)
Async XLA Ops:
  0.6 13.4 %collective-permute-start.3 = (bf16[1002,4096]{1,0:T(8,128)(2,1)}, bf16[1002,4096]{1,0:T(8,128)(2,1)}, u32[]{:S(2)}, u32[]{:S(2)}) collective-permute-start(bf16[1002,4096]{1,0:T(8,128)(2,1)} %bitcast.95), channel_id=1, source_target_pairs={{0,8},{8,0},{1,9},{9,1},{2,10},{10,2},{3,11},{11,3},{4,12},{12,4},... | collective-permute-start | bytes 24625160 | tf_op jit(solution)/shard_map/ppermute | solution.py:25
  2.4 9.5 %collective-permute-start = (bf16[2,2,48,256]{3,2,1,0:T(8,128)(2,1)S(1)}, bf16[2,2,48,256]{3,2,1,0:T(8,128)(2,1)S(1)}, u32[]{:S(2)}, u32[]{:S(2)}) collective-permute-start(bf16[2,2,48,256]{3,2,1,0:T(8,128)(2,1)S(1)} %bitcast.90), channel_id=1, source_target_pairs={{0,2},{2,4},{4,6},{6,0},{1,3},{3,5},{5,7},{7,1},{8,10},{10,12},{12... | collective-permute-start | bytes 294920 | tf_op jit(solution)/shard_map/ppermute | solution.py:21
  4.5 8.9 %collective-permute-start.1 = (bf16[2,2,48,256]{3,2,1,0:T(8,128)(2,1)S(1)}, bf16[2,2,48,256]{3,2,1,0:T(8,128)(2,1)S(1)}, u32[]{:S(2)}, u32[]{:S(2)}) collective-permute-start(bf16[2,2,48,256]{3,2,1,0:T(8,128)(2,1)S(1)} %bitcast.91), channel_id=1, source_target_pairs={{0,4},{2,6},{4,0},{6,2},{1,5},{3,7},{5,1},{7,3},{8,12},{10,14},{12... | collective-permute-start | bytes 294920 | tf_op jit(solution)/shard_map/ppermute | solution.py:21
  8.0 5.3 %collective-permute-start.2 = (bf16[2,2,48,256]{3,2,1,0:T(8,128)(2,1)S(1)}, bf16[2,2,48,256]{3,2,1,0:T(8,128)(2,1)S(1)}, u32[]{:S(2)}, u32[]{:S(2)}) collective-permute-start(bf16[2,2,48,256]{3,2,1,0:T(8,128)(2,1)S(1)} %bitcast.92), channel_id=1, source_target_pairs={{0,6},{2,0},{4,2},{6,4},{1,7},{3,1},{5,3},{7,5},{8,14},{10,8},{12,... | collective-permute-start | bytes 294920 | tf_op jit(solution)/shard_map/ppermute | solution.py:21
  14.1 10.5 %collective-permute-start.7 = (bf16[384,256]{1,0:T(8,128)(2,1)S(1)}, bf16[384,256]{1,0:T(8,128)(2,1)S(1)}, u32[]{:S(2)}, u32[]{:S(2)}) collective-permute-start(bf16[384,256]{1,0:T(8,128)(2,1)S(1)} %pad_maximum_fusion), channel_id=1, source_target_pairs={{0,1},{1,64},{64,65},{65,0},{2,3},{3,66},{66,67},{67,2},{4,5},{5,6... | collective-permute-start | bytes 589832 | tf_op jit(solution)/shard_map/ppermute | solution.py:21
  15.8 12.0 %collective-permute-start.8 = (bf16[384,256]{1,0:T(8,128)(2,1)S(1)}, bf16[384,256]{1,0:T(8,128)(2,1)S(1)}, u32[]{:S(2)}, u32[]{:S(2)}) collective-permute-start(bf16[384,256]{1,0:T(8,128)(2,1)S(1)} %pad_maximum_fusion), channel_id=1, source_target_pairs={{0,64},{1,65},{64,0},{65,1},{2,66},{3,67},{66,2},{67,3},{4,68},{5,... | collective-permute-start | bytes 589832 | tf_op jit(solution)/shard_map/ppermute | solution.py:21
  18.7 9.2 %collective-permute-start.9 = (bf16[384,256]{1,0:T(8,128)(2,1)S(1)}, bf16[384,256]{1,0:T(8,128)(2,1)S(1)}, u32[]{:S(2)}, u32[]{:S(2)}) collective-permute-start(bf16[384,256]{1,0:T(8,128)(2,1)S(1)} %pad_maximum_fusion), channel_id=1, source_target_pairs={{0,65},{1,0},{64,1},{65,64},{2,67},{3,2},{66,3},{67,66},{4,69},{5,... | collective-permute-start | bytes 589832 | tf_op jit(solution)/shard_map/ppermute | solution.py:21
  20.1 8.3 %collective-permute-start.4 = (bf16[400,256]{1,0:T(8,128)(2,1)S(1)}, bf16[400,256]{1,0:T(8,128)(2,1)S(1)}, u32[]{:S(2)}, u32[]{:S(2)}) collective-permute-start(bf16[400,256]{1,0:T(8,128)(2,1)S(1)} %fusion.3), channel_id=1, source_target_pairs={{0,16},{16,32},{32,48},{48,0},{1,17},{17,33},{33,49},{49,1},{2,18}... | collective-permute-start | bytes 614408 | tf_op jit(solution)/shard_map/ppermute | solution.py:21
  21.6 11.4 %collective-permute-start.5 = (bf16[400,256]{1,0:T(8,128)(2,1)S(1)}, bf16[400,256]{1,0:T(8,128)(2,1)S(1)}, u32[]{:S(2)}, u32[]{:S(2)}) collective-permute-start(bf16[400,256]{1,0:T(8,128)(2,1)S(1)} %fusion.3), channel_id=1, source_target_pairs={{0,32},{16,48},{32,0},{48,16},{1,33},{17,49},{33,1},{49,17},{2,34}... | collective-permute-start | bytes 614408 | tf_op jit(solution)/shard_map/ppermute | solution.py:21
  24.6 8.5 %collective-permute-start.6 = (bf16[400,256]{1,0:T(8,128)(2,1)S(1)}, bf16[400,256]{1,0:T(8,128)(2,1)S(1)}, u32[]{:S(2)}, u32[]{:S(2)}) collective-permute-start(bf16[400,256]{1,0:T(8,128)(2,1)S(1)} %fusion.3), channel_id=1, source_target_pairs={{0,48},{16,0},{32,16},{48,32},{1,49},{17,1},{33,17},{49,33},{2,50}... | collective-permute-start | bytes 614408 | tf_op jit(solution)/shard_map/ppermute | solution.py:21
  33.1 23.5 %copy-start.2 = (bf16[4,208,256]{2,1,0:T(8,128)(2,1)}, bf16[4,208,256]{2,1,0:T(8,128)(2,1)S(1)}, u32[]{:S(2)}) copy-start(bf16[4,208,256]{2,1,0:T(8,128)(2,1)S(1)} %slice.94.refs_0_) | copy-start | bytes 1277956
  33.1 14.9 %collective-permute-start.11 = (bf16[4,208,256]{2,1,0:T(8,128)(2,1)S(1)}, bf16[4,208,256]{2,1,0:T(8,128)(2,1)S(1)}, u32[]{:S(2)}, u32[]{:S(2)}) collective-permute-start(bf16[4,208,256]{2,1,0:T(8,128)(2,1)S(1)} %slice.94.refs_0_), channel_id=1, source_target_pairs={{0,1},{1,64},{64,65},{65,0},{2,3},{3,66},{66,67},{67,2},{4,5},{5,6... | collective-permute-start | bytes 1277960 | tf_op jit(solution)/shard_map/ppermute | solution.py:21
  33.9 14.1 %collective-permute-start.12 = (bf16[4,208,256]{2,1,0:T(8,128)(2,1)S(1)}, bf16[4,208,256]{2,1,0:T(8,128)(2,1)S(1)}, u32[]{:S(2)}, u32[]{:S(2)}) collective-permute-start(bf16[4,208,256]{2,1,0:T(8,128)(2,1)S(1)} %slice.94.refs_0_), channel_id=1, source_target_pairs={{0,65},{1,0},{64,1},{65,64},{2,67},{3,2},{66,3},{67,66},{4,69},{5,... | collective-permute-start | bytes 1277960 | tf_op jit(solution)/shard_map/ppermute | solution.py:21
  36.5 12.6 %copy-start.3 = (bf16[4,192,256]{2,1,0:T(8,128)(2,1)}, bf16[4,192,256]{2,1,0:T(8,128)(2,1)S(1)}, u32[]{:S(2)}) copy-start(bf16[4,192,256]{2,1,0:T(8,128)(2,1)S(1)} %get-tuple-element.71.refs_4_) | copy-start | bytes 1179652
  36.5 10.1 %collective-permute-start.13 = (bf16[4,192,256]{2,1,0:T(8,128)(2,1)S(1)}, bf16[4,192,256]{2,1,0:T(8,128)(2,1)S(1)}, u32[]{:S(2)}, u32[]{:S(2)}) collective-permute-start(bf16[4,192,256]{2,1,0:T(8,128)(2,1)S(1)} %get-tuple-element.71.refs_4_), channel_id=1, source_target_pairs={{0,16},{16,32},{32,48},{48,0},{1,17},{17,33},{33,49},{49,1},{2,18}... | collective-permute-start | bytes 1179656 | tf_op jit(solution)/shard_map/ppermute | solution.py:21
  38.2 9.8 %collective-permute-start.14 = (bf16[4,192,256]{2,1,0:T(8,128)(2,1)S(1)}, bf16[4,192,256]{2,1,0:T(8,128)(2,1)S(1)}, u32[]{:S(2)}, u32[]{:S(2)}) collective-permute-start(bf16[4,192,256]{2,1,0:T(8,128)(2,1)S(1)} %get-tuple-element.71.refs_4_), channel_id=1, source_target_pairs={{0,48},{16,0},{32,16},{48,32},{1,49},{17,1},{33,17},{49,33},{2,50}... | collective-permute-start | bytes 1179656 | tf_op jit(solution)/shard_map/ppermute | solution.py:21
  39.8 23.5 %copy-start.1 = (bf16[4,192,256]{2,1,0:T(8,128)(2,1)}, bf16[4,192,256]{2,1,0:T(8,128)(2,1)S(1)}, u32[]{:S(2)}) copy-start(bf16[4,192,256]{2,1,0:T(8,128)(2,1)S(1)} %slice.100.refs_0_) | copy-start | bytes 1179652
  46.6 2.3 %copy-start.7 = (bf16[4,192,256]{2,1,0:T(8,128)(2,1)}, bf16[4,192,256]{2,1,0:T(8,128)(2,1)S(1)}, u32[]{:S(2)}) copy-start(bf16[4,192,256]{2,1,0:T(8,128)(2,1)S(1)} %collective-permute-done.13.refs_5_) | copy-start | bytes 1179652
  48.0 0.9 copy-start.8
  48.0 1.1 copy-start.5
  48.0 0.9 copy-start.6
  48.9 32.6 %collective-permute-start.19 = (bf16[1002,4096]{1,0:T(8,128)(2,1)}, bf16[1002,4096]{1,0:T(8,128)(2,1)}, u32[]{:S(2)}, u32[]{:S(2)}) collective-permute-start(bf16[1002,4096]{1,0:T(8,128)(2,1)} %bitcast.26.refs_8_), channel_id=1, source_target_pairs={{0,8},{8,0},{1,9},{9,1},{2,10},{10,2},{3,11},{11,3},{4,12},{12,4},... | collective-permute-start | bytes 24625160 | tf_op jit(solution)/shard_map/ppermute | solution.py:25
  48.9 14.4 %collective-permute-start.10 = (bf16[4,208,256]{2,1,0:T(8,128)(2,1)S(1)}, bf16[4,208,256]{2,1,0:T(8,128)(2,1)}, u32[]{:S(2)}, u32[]{:S(2)}) collective-permute-start(bf16[4,208,256]{2,1,0:T(8,128)(2,1)S(1)} %slice.94.refs_0_), channel_id=1, source_target_pairs={{0,64},{1,65},{64,0},{65,1},{2,66},{3,67},{66,2},{67,3},{4,68},{5,... | collective-permute-start | bytes 1277960 | tf_op jit(solution)/shard_map/ppermute | solution.py:21
  50.1 15.6 %collective-permute-start.15 = (bf16[4,192,256]{2,1,0:T(8,128)(2,1)}, bf16[4,192,256]{2,1,0:T(8,128)(2,1)}, u32[]{:S(2)}, u32[]{:S(2)}) collective-permute-start(bf16[4,192,256]{2,1,0:T(8,128)(2,1)} %copy-done.3), channel_id=1, source_target_pairs={{0,32},{16,48},{32,0},{48,16},{1,33},{17,49},{33,1},{49,17},{2,34}... | collective-permute-start | bytes 1179656 | tf_op jit(solution)/shard_map/ppermute | solution.py:21
  52.0 29.4 %collective-permute-start.16 = (bf16[4,192,256]{2,1,0:T(8,128)(2,1)S(1)}, bf16[4,192,256]{2,1,0:T(8,128)(2,1)}, u32[]{:S(2)}, u32[]{:S(2)}) collective-permute-start(bf16[4,192,256]{2,1,0:T(8,128)(2,1)S(1)} %slice.100.refs_0_), channel_id=1, source_target_pairs={{0,1},{1,64},{64,65},{65,0},{2,3},{3,66},{66,67},{67,2},{4,5},{5,6... | collective-permute-start | bytes 1179656 | tf_op jit(solution)/shard_map/ppermute | solution.py:21
  52.9 28.5 %collective-permute-start.17 = (bf16[4,192,256]{2,1,0:T(8,128)(2,1)S(1)}, bf16[4,192,256]{2,1,0:T(8,128)(2,1)}, u32[]{:S(2)}, u32[]{:S(2)}) collective-permute-start(bf16[4,192,256]{2,1,0:T(8,128)(2,1)S(1)} %slice.100.refs_0_), channel_id=1, source_target_pairs={{0,64},{1,65},{64,0},{65,1},{2,66},{3,67},{66,2},{67,3},{4,68},{5,... | collective-permute-start | bytes 1179656 | tf_op jit(solution)/shard_map/ppermute | solution.py:21
  56.6 24.8 %all-to-all-start = ((bf16[4,4,192,256]{3,2,1,0:T(8,128)(2,1)}), bf16[4,4,192,256]{3,2,1,0:T(8,128)(2,1)S(1)}, u32[]{:S(2)}, u32[]{:S(2)}) async-start(bf16[4,4,192,256]{3,2,1,0:T(8,128)(2,1)} %broadcast_in_dim.85), calls=%async_computation | async-start | bytes 3145728 | tf_op jit(solution)/shard_map/all_to_all | solution.py:263
  63.3 18.1 %collective-permute-start.18 = (bf16[4,192,256]{2,1,0:T(8,128)(2,1)S(1)}, bf16[4,192,256]{2,1,0:T(8,128)(2,1)S(1)}, u32[]{:S(2)}, u32[]{:S(2)}) collective-permute-start(bf16[4,192,256]{2,1,0:T(8,128)(2,1)S(1)} %slice.100.refs_0_), channel_id=1, source_target_pairs={{0,65},{1,0},{64,1},{65,64},{2,67},{3,2},{66,3},{67,66},{4,69},{5,... | collective-permute-start | bytes 1179656 | tf_op jit(solution)/shard_map/ppermute | solution.py:21
  81.4 0.7 copy-start.4
  81.5 1.3 copy-start
  97.6 23.3 %all-to-all-start.1 = ((f32[64,8,384]{2,1,0:T(8,128)}), f32[64,8,384]{2,1,0:T(8,128)S(1)}, u32[]{:S(2)}, u32[]{:S(2)}) async-start(f32[64,8,384]{2,1,0:T(8,128)} %get-tuple-element.50), calls=%async_computation.1 | async-start | bytes 1572864 | tf_op jit(solution)/shard_map/all_to_all | solution.py:292
  106.8 39.7 %collective-permute-start.21 = (bf16[384,4096]{1,0:T(8,128)(2,1)}, bf16[384,4096]{1,0:T(8,128)(2,1)}, u32[]{:S(2)}, u32[]{:S(2)}) collective-permute-start(bf16[384,4096]{1,0:T(8,128)(2,1)} %get-tuple-element.58.hidden_a), channel_id=1, source_target_pairs={{0,8},{8,0},{1,9},{9,1},{2,10},{10,2},{3,11},{11,3},{4,12},{12,4},... | collective-permute-start | bytes 9437192 | tf_op jit(solution)/shard_map/ppermute | solution.py:25
  137.5 44.6 %all-to-all-start.2 = ((bf16[64,48,512]{2,1,0:T(8,128)(2,1)}), bf16[64,48,512]{2,1,0:T(8,128)(2,1)S(1)}, u32[]{:S(2)}, u32[]{:S(2)}) async-start(bf16[64,48,512]{2,1,0:T(8,128)(2,1)} %bitcast.81), calls=%async_computation.2 | async-start | bytes 6291456 | tf_op jit(solution)/shard_map/all_to_all | solution.py:321
  143.4 3.1 %collective-permute-start.20 = (bf16[1002,384]{1,0:T(8,128)(2,1)}, bf16[1002,384]{1,0:T(8,128)(2,1)}, u32[]{:S(2)}, u32[]{:S(2)}) collective-permute-start(bf16[1002,384]{1,0:T(8,128)(2,1)} %get-tuple-element.57), channel_id=1, source_target_pairs={{0,8},{8,0},{1,9},{9,1},{2,10},{10,2},{3,11},{11,3},{4,12},{12,4},... | collective-permute-start | bytes 2308616 | tf_op jit(solution)/shard_map/ppermute | solution.py:25
  144.3 1.7 collective-permute-start.22

commit v4 on v3

--- a/solution.py
+++ b/solution.py
@@ -39,6 +39,7 @@
 
 
 VMEM_LIMIT = 60 * 1024 * 1024
+Q_VMEM_LIMIT = 52 * 1024 * 1024
 NT = (((1,), (1,)), ((), ()))
 NN = (((1,), (0,)), ((), ()))
 
@@ -145,7 +146,7 @@
         out_specs=out_specs,
         out_shape=outs,
         scratch_shapes=scratch,
-        compiler_params=pltpu.CompilerParams(vmem_limit_bytes=VMEM_LIMIT),
+        compiler_params=pltpu.CompilerParams(vmem_limit_bytes=Q_VMEM_LIMIT),
         cost_estimate=cost(
             4 * tokens * width * feats_all, 4 * width * feats_all + 2 * tokens * feats_all, 2 * tokens * width
         ),
@@ -241,7 +242,8 @@
     extra = jnp.concatenate([v.astype(bf16) for v in extra])
     extra = jnp.pad(extra[None], ((0, 15), (0, half - extra.shape[0])))
 
-    both = jnp.stack([learn_hidden, target_hidden]).reshape(2, rows, 2, half).transpose(2, 0, 1, 3)
+    both = [v[:, at : at + half] for at in (0, half) for v in (learn_hidden, target_hidden)]
+    both = jnp.stack(both).reshape(2, 2, rows, half)
     both, learn_sib = lax.optimization_barrier((gather_ring(both, "z"), learn_sib))
     block = 4 * rows
     first, second = (

time: 184 us -> 181 us (0.984)
  local copies, waits for them, and re-layouts: 8.93 us -> 6.2 us
  transfers between devices with their start and end apart: 26 -> 26, of which waited for: 11 -> 11; matrix products, arithmetic and copies ran while one was open for 7% -> 6% of each run, Pallas kernels for 23% -> 23%
where the time goes in v4:
time: 181 us
  waiting for transfers between devices  58.3 us (32%)
  Pallas kernels  57 us (31%)
  starting transfers between devices  50.4 us (28%)
  other arithmetic  7.39 us (4%)
  local copies, waits for them, and re-layouts  6.2 us (3%)
    ppermute x18, starting transfers between devices, shift(): return lax.ppermute(v, axis, [(i, (i + by) % 4) for i in range(4)])  30.5 us
    pallas_call x2, Pallas kernels, q_values(): pl.pallas_call(functools.partial(q_kernel, learner), grid=(feats_all // (...  30 us
    all_to_all x1, waiting for transfers between devices, shards(): lax.all_to_all(partial.reshape(64, rows, feats), PLANE, 0, 0, tiled=True)  22.9 us
    ppermute x18, waiting for transfers between devices, shift(): return lax.ppermute(v, axis, [(i, (i + by) % 4) for i in range(4)])  19.3 us
    pallas_call x1, Pallas kernels, gradients(): pl.pallas_call(functools.partial(grad_kernel, 1.0 / traj_total), grid=(fe...  14.5 us
    all_to_all x1, waiting for transfers between devices, shards(): packed = lax.all_to_all(target_stats, PLANE, 0, 0, tiled=True)  13.4 us
    pallas_call x1, Pallas kernels, head_gradient(): pl.pallas_call(head_kernel, grid=(4,), in_specs=[whole((width, tokens))]...  12.5 us
    all_to_all x1, starting transfers between devices, shards(): packed = lax.all_to_all(target_stats, PLANE, 0, 0, tiled=True)  8.68 us
  transfers between devices with their start and end apart: 26, of which 11 were waited for; matrix products, arithmetic and copies ran while one was open for 6% of the time, Pallas kernels for 23%

profile of v4, /device:TPU:0, one launch (start us, length us, event | category | flops | bytes accessed | tf_op | source)
XLA Modules:
  0.0 180.5 jit_solution(11505484803970413064)
XLA Ops:
  0.7 0.8 slice_bitcast_fusion.2
  1.5 2.1 %collective-permute-start = (bf16[2,2,48,256]{3,2,1,0:T(8,128)(2,1)S(1)}, bf16[2,2,48,256]{3,2,1,0:T(8,128)(2,1)S(1)}, u32[]{:S(2)}, u32[]{:S(2)}) collective-permute-start(bf16[2,2,48,256]{3,2,1,0:T(8,128)(2,1)S(1)} %bitcast.96), channel_id=1, source_target_pairs={{0,2},{2,4},{4,6},{6,0},{1,3},{3,5},{5,7},{7,1},{8,10},{10,12},{12... | collective-permute-start | bytes 294920 | tf_op jit(solution)/shard_map/ppermute | solution.py:21
  3.6 3.6 %collective-permute-start.1 = (bf16[2,2,48,256]{3,2,1,0:T(8,128)(2,1)S(1)}, bf16[2,2,48,256]{3,2,1,0:T(8,128)(2,1)S(1)}, u32[]{:S(2)}, u32[]{:S(2)}) collective-permute-start(bf16[2,2,48,256]{3,2,1,0:T(8,128)(2,1)S(1)} %bitcast.97), channel_id=1, source_target_pairs={{0,4},{2,6},{4,0},{6,2},{1,5},{3,7},{5,1},{7,3},{8,12},{10,14},{12... | collective-permute-start | bytes 294920 | tf_op jit(solution)/shard_map/ppermute | solution.py:21
  7.2 1.0 collective-permute-start.2
  8.2 0.7 convert_element_type.49
  8.9 0.7 convert_element_type.50
  9.5 0.7 shift-right-arithmetic_convert_fusion
  10.2 0.8 concatenate.33
  11.0 1.4 collective-permute-done.1
  12.5 1.5 collective-permute-done.3.refs_9_.sib_ref
  14.1 1.7 collective-permute-start.7
  15.8 2.9 %collective-permute-start.8 = (bf16[384,256]{1,0:T(8,128)(2,1)S(1)}, bf16[384,256]{1,0:T(8,128)(2,1)S(1)}, u32[]{:S(2)}, u32[]{:S(2)}) collective-permute-start(bf16[384,256]{1,0:T(8,128)(2,1)S(1)} %pad_maximum_fusion), channel_id=1, source_target_pairs={{0,64},{1,65},{64,0},{65,1},{2,66},{3,67},{66,2},{67,3},{4,68},{5,... | collective-permute-start | bytes 589832 | tf_op jit(solution)/shard_map/ppermute | solution.py:21
  18.7 1.3 collective-permute-start.9
  20.1 1.6 collective-permute-start.4
  21.6 2.7 %collective-permute-start.5 = (bf16[400,256]{1,0:T(8,128)(2,1)S(1)}, bf16[400,256]{1,0:T(8,128)(2,1)S(1)}, u32[]{:S(2)}, u32[]{:S(2)}) collective-permute-start(bf16[400,256]{1,0:T(8,128)(2,1)S(1)} %fusion.3), channel_id=1, source_target_pairs={{0,32},{16,48},{32,0},{48,16},{1,33},{17,49},{33,1},{49,17},{2,34}... | collective-permute-start | bytes 614408 | tf_op jit(solution)/shard_map/ppermute | solution.py:21
  24.6 1.5 collective-permute-start.6
  26.1 1.8 collective-permute-done.8
  28.4 4.6 %collective-permute-done.5 = bf16[400,256]{1,0:T(8,128)(2,1)S(1)} collective-permute-done((bf16[400,256]{1,0:T(8,128)(2,1)S(1)}, bf16[400,256]{1,0:T(8,128)(2,1)S(1)}, u32[]{:S(2)}, u32[]{:S(2)}) %collective-permute-start.5) | collective-permute-done | bytes 204832 | tf_op jit(solution)/shard_map/ppermute | solution.py:21
  33.1 0.7 collective-permute-start.11
  33.8 2.6 %collective-permute-start.12 = (bf16[4,208,256]{2,1,0:T(8,128)(2,1)S(1)}, bf16[4,208,256]{2,1,0:T(8,128)(2,1)S(1)}, u32[]{:S(2)}, u32[]{:S(2)}) collective-permute-start(bf16[4,208,256]{2,1,0:T(8,128)(2,1)S(1)} %slice.110.refs_0_), channel_id=1, source_target_pairs={{0,65},{1,0},{64,1},{65,64},{2,67},{3,2},{66,3},{67,66},{4,69},{5,... | collective-permute-start | bytes 1277960 | tf_op jit(solution)/shard_map/ppermute | solution.py:21
  36.5 1.7 collective-permute-start.13
  38.2 1.6 collective-permute-start.14
  39.8 6.8 %collective-permute-done.13.refs_5_ = bf16[4,192,256]{2,1,0:T(8,128)(2,1)S(1)} collective-permute-done((bf16[4,192,256]{2,1,0:T(8,128)(2,1)S(1)}, bf16[4,192,256]{2,1,0:T(8,128)(2,1)S(1)}, u32[]{:S(2)}, u32[]{:S(2)}) %collective-permute-start.13) | collective-permute-done | bytes 393248 | tf_op jit(solution)/shard_map/ppermute | solution.py:21
  46.6 1.4 collective-permute-done.14.refs_7_
  48.0 0.8 copy-done.2
  49.5 1.9 %collective-permute-start.15 = (bf16[4,192,256]{2,1,0:T(8,128)(2,1)S(1)}, bf16[4,192,256]{2,1,0:T(8,128)(2,1)}, u32[]{:S(2)}, u32[]{:S(2)}) collective-permute-start(bf16[4,192,256]{2,1,0:T(8,128)(2,1)S(1)} %get-tuple-element.71.refs_4_), channel_id=1, source_target_pairs={{0,32},{16,48},{32,0},{48,16},{1,33},{17,49},{33,1},{49,17},{2,34}... | collective-permute-start | bytes 1179656 | tf_op jit(solution)/shard_map/ppermute | solution.py:21
  51.5 0.8 collective-permute-start.16
  52.2 2.5 %collective-permute-start.17 = (bf16[4,192,256]{2,1,0:T(8,128)(2,1)S(1)}, bf16[4,192,256]{2,1,0:T(8,128)(2,1)S(1)}, u32[]{:S(2)}, u32[]{:S(2)}) collective-permute-start(bf16[4,192,256]{2,1,0:T(8,128)(2,1)S(1)} %slice.116.refs_0_), channel_id=1, source_target_pairs={{0,64},{1,65},{64,0},{65,1},{2,66},{3,67},{66,2},{67,3},{4,68},{5,... | collective-permute-start | bytes 1179656 | tf_op jit(solution)/shard_map/ppermute | solution.py:21
  54.7 1.3 broadcast_in_dim.85
  56.0 4.4 %all-to-all-start = ((bf16[4,4,192,256]{3,2,1,0:T(8,128)(2,1)}), bf16[4,4,192,256]{3,2,1,0:T(8,128)(2,1)}, u32[]{:S(2)}, u32[]{:S(2)}) async-start(bf16[4,4,192,256]{3,2,1,0:T(8,128)(2,1)} %broadcast_in_dim.85), calls=%async_computation | async-start | bytes 3145728 | tf_op jit(solution)/shard_map/all_to_all | solution.py:265
  60.4 2.9 %collective-permute-done.10.refs_2_ = bf16[4,208,256]{2,1,0:T(8,128)(2,1)} collective-permute-done((bf16[4,208,256]{2,1,0:T(8,128)(2,1)S(1)}, bf16[4,208,256]{2,1,0:T(8,128)(2,1)}, u32[]{:S(2)}, u32[]{:S(2)}) %collective-permute-start.10) | collective-permute-done | bytes 426016 | tf_op jit(solution)/shard_map/ppermute | solution.py:21
  63.5 0.7 broadcast_select_fusion
  64.2 0.7 slice_convert_fusion
  65.0 0.7 fusion.36
  65.8 15.4 %shard_map.103 = (f32[384,1002]{1,0:T(8,128)}, f32[384,1002]{1,0:T(8,128)}, f32[8,384]{1,0:T(8,128)S(1)}, bf16[384,4096]{1,0:T(8,128)(2,1)}) custom-call(s32[4]{0:T(128)S(1)} %pad_add_fusion.ids_ref, f32[8,384]{1,0:T(8,128)S(1)} %scatter.4.vec_ref, bf16[4,208,256]{2,1,0:T(8,128)(2,1)S(1)} %slice.110.refs_0_, bf16[4,208,256]{2,1,0:T(8,128)(2,1)} %copy-done.2, ...), custom_call_target="tpu_custom_call" | custom-call | flops 6304038912 | bytes 19562496 | tf_op jit(solution)/shard_map/pallas_call | solution.py:142
  81.3 14.7 %shard_map.104 = (f32[384,1002]{1,0:T(8,128)}, f32[384,1002]{1,0:T(8,128)}, f32[64,8,384]{2,1,0:T(8,128)}) custom-call(s32[4]{0:T(128)S(1)} %pad_add_fusion.ids_ref, f32[8,384]{1,0:T(8,128)S(1)} %get-tuple-element.46.vec_ref, bf16[4,192,256]{2,1,0:T(8,128)(2,1)S(1)} %slice.116.refs_0_, bf16[4,192,256]{2,1,0:T(8,128)(2,1)S(1)} %collective-permute-done.16.refs_1_, ...), custom_call_target="tpu_custom_call" | custom-call | flops 6304038912 | bytes 19562496 | tf_op jit(solution)/shard_map/pallas_call | solution.py:142
  95.9 8.7 %all-to-all-start.1 = ((f32[64,8,384]{2,1,0:T(8,128)}), f32[64,8,384]{2,1,0:T(8,128)S(1)}, u32[]{:S(2)}, u32[]{:S(2)}) async-start(f32[64,8,384]{2,1,0:T(8,128)} %get-tuple-element.50), calls=%async_computation.1 | async-start | bytes 1572864 | tf_op jit(solution)/shard_map/all_to_all | solution.py:294
  105.1 13.4 %all-to-all-done.1 = f32[64,8,384]{2,1,0:T(8,128)S(1)} async-done(((f32[64,8,384]{2,1,0:T(8,128)}), f32[64,8,384]{2,1,0:T(8,128)S(1)}, u32[]{:S(2)}, u32[]{:S(2)}) %all-to-all-start.1) | async-done | bytes 786464 | tf_op jit(solution)/shard_map/all_to_all | solution.py:294
  119.1 0.8 subtract_select_fusion
  119.9 0.6 concatenate.39.vec_ref
  120.5 14.5 %shard_map.105 = (bf16[1002,384]{1,0:T(8,128)(2,1)}, bf16[1002,384]{1,0:T(8,128)(2,1)}, bf16[8,8,48,512]{3,2,1,0:T(8,128)(2,1)}) custom-call(s32[4]{0:T(128)} %copy-done, f32[8,384]{1,0:T(8,128)} %concatenate.39.vec_ref, f32[384,1002]{1,0:T(8,128)} %get-tuple-element.51.le_own, f32[384,1002]{1,0:T(8,128)} %get-tuple-element.52.le_sib, ...), custom_call_target="tpu_custom_call" | custom-call | flops 6304038912 | bytes 19562496 | tf_op jit(solution)/shard_map/pallas_call | solution.py:188
  135.0 5.9 %all-to-all-start.2 = ((bf16[64,48,512]{2,1,0:T(8,128)(2,1)}), bf16[64,48,512]{2,1,0:T(8,128)(2,1)S(1)}, u32[]{:S(2)}, u32[]{:S(2)}) async-start(bf16[64,48,512]{2,1,0:T(8,128)(2,1)} %bitcast.87), calls=%async_computation.2 | async-start | bytes 6291456 | tf_op jit(solution)/shard_map/all_to_all | solution.py:323
  141.8 0.5 collective-permute-start.22
  142.4 1.1 collective-permute-done.22
  143.5 0.5 fusion.51
  144.0 12.5 %shard_map.106 = bf16[1002,4096]{1,0:T(8,128)(2,1)} custom-call(bf16[1002,384]{1,0:T(8,128)(2,1)} %get-tuple-element.56.grad_a, bf16[1002,384]{1,0:T(8,128)(2,1)} %collective-permute-done.20.grad_b, bf16[384,4096]{1,0:T(8,128)(2,1)} %get-tuple-element.58.hidden_a, bf16[384,4096]{1,0:T(8,128)(2,1)} %collective-permute-done.21.hidden_b), custom_call_target="tpu_custom_call" | custom-call | flops 6304038912 | bytes 14499840 | tf_op jit(solution)/shard_map/pallas_call | solution.py:216
  156.5 22.9 %all-to-all-done.2 = bf16[64,48,512]{2,1,0:T(8,128)(2,1)S(1)} async-done(((bf16[64,48,512]{2,1,0:T(8,128)(2,1)}), bf16[64,48,512]{2,1,0:T(8,128)(2,1)S(1)}, u32[]{:S(2)}, u32[]{:S(2)}) %all-to-all-start.2) | async-done | bytes 3145760 | tf_op jit(solution)/shard_map/all_to_all | solution.py:323
  179.4 1.1 reduce_sum.53
  (77 shorter events, 4.2 us)
Async XLA Ops:
  0.6 13.4 %collective-permute-start.3 = (bf16[1002,4096]{1,0:T(8,128)(2,1)}, bf16[1002,4096]{1,0:T(8,128)(2,1)}, u32[]{:S(2)}, u32[]{:S(2)}) collective-permute-start(bf16[1002,4096]{1,0:T(8,128)(2,1)} %bitcast.102), channel_id=1, source_target_pairs={{0,8},{8,0},{1,9},{9,1},{2,10},{10,2},{3,11},{11,3},{4,12},{12,4},... | collective-permute-start | bytes 24625160 | tf_op jit(solution)/shard_map/ppermute | solution.py:25
  1.5 9.5 %collective-permute-start = (bf16[2,2,48,256]{3,2,1,0:T(8,128)(2,1)S(1)}, bf16[2,2,48,256]{3,2,1,0:T(8,128)(2,1)S(1)}, u32[]{:S(2)}, u32[]{:S(2)}) collective-permute-start(bf16[2,2,48,256]{3,2,1,0:T(8,128)(2,1)S(1)} %bitcast.96), channel_id=1, source_target_pairs={{0,2},{2,4},{4,6},{6,0},{1,3},{3,5},{5,7},{7,1},{8,10},{10,12},{12... | collective-permute-start | bytes 294920 | tf_op jit(solution)/shard_map/ppermute | solution.py:21
  3.6 8.9 %collective-permute-start.1 = (bf16[2,2,48,256]{3,2,1,0:T(8,128)(2,1)S(1)}, bf16[2,2,48,256]{3,2,1,0:T(8,128)(2,1)S(1)}, u32[]{:S(2)}, u32[]{:S(2)}) collective-permute-start(bf16[2,2,48,256]{3,2,1,0:T(8,128)(2,1)S(1)} %bitcast.97), channel_id=1, source_target_pairs={{0,4},{2,6},{4,0},{6,2},{1,5},{3,7},{5,1},{7,3},{8,12},{10,14},{12... | collective-permute-start | bytes 294920 | tf_op jit(solution)/shard_map/ppermute | solution.py:21
  7.2 5.3 %collective-permute-start.2 = (bf16[2,2,48,256]{3,2,1,0:T(8,128)(2,1)S(1)}, bf16[2,2,48,256]{3,2,1,0:T(8,128)(2,1)S(1)}, u32[]{:S(2)}, u32[]{:S(2)}) collective-permute-start(bf16[2,2,48,256]{3,2,1,0:T(8,128)(2,1)S(1)} %bitcast.98), channel_id=1, source_target_pairs={{0,6},{2,0},{4,2},{6,4},{1,7},{3,1},{5,3},{7,5},{8,14},{10,8},{12,... | collective-permute-start | bytes 294920 | tf_op jit(solution)/shard_map/ppermute | solution.py:21
  14.1 10.5 %collective-permute-start.7 = (bf16[384,256]{1,0:T(8,128)(2,1)S(1)}, bf16[384,256]{1,0:T(8,128)(2,1)S(1)}, u32[]{:S(2)}, u32[]{:S(2)}) collective-permute-start(bf16[384,256]{1,0:T(8,128)(2,1)S(1)} %pad_maximum_fusion), channel_id=1, source_target_pairs={{0,1},{1,64},{64,65},{65,0},{2,3},{3,66},{66,67},{67,2},{4,5},{5,6... | collective-permute-start | bytes 589832 | tf_op jit(solution)/shard_map/ppermute | solution.py:21
  15.8 12.0 %collective-permute-start.8 = (bf16[384,256]{1,0:T(8,128)(2,1)S(1)}, bf16[384,256]{1,0:T(8,128)(2,1)S(1)}, u32[]{:S(2)}, u32[]{:S(2)}) collective-permute-start(bf16[384,256]{1,0:T(8,128)(2,1)S(1)} %pad_maximum_fusion), channel_id=1, source_target_pairs={{0,64},{1,65},{64,0},{65,1},{2,66},{3,67},{66,2},{67,3},{4,68},{5,... | collective-permute-start | bytes 589832 | tf_op jit(solution)/shard_map/ppermute | solution.py:21
  18.7 9.2 %collective-permute-start.9 = (bf16[384,256]{1,0:T(8,128)(2,1)S(1)}, bf16[384,256]{1,0:T(8,128)(2,1)S(1)}, u32[]{:S(2)}, u32[]{:S(2)}) collective-permute-start(bf16[384,256]{1,0:T(8,128)(2,1)S(1)} %pad_maximum_fusion), channel_id=1, source_target_pairs={{0,65},{1,0},{64,1},{65,64},{2,67},{3,2},{66,3},{67,66},{4,69},{5,... | collective-permute-start | bytes 589832 | tf_op jit(solution)/shard_map/ppermute | solution.py:21
  20.1 8.3 %collective-permute-start.4 = (bf16[400,256]{1,0:T(8,128)(2,1)S(1)}, bf16[400,256]{1,0:T(8,128)(2,1)S(1)}, u32[]{:S(2)}, u32[]{:S(2)}) collective-permute-start(bf16[400,256]{1,0:T(8,128)(2,1)S(1)} %fusion.3), channel_id=1, source_target_pairs={{0,16},{16,32},{32,48},{48,0},{1,17},{17,33},{33,49},{49,1},{2,18}... | collective-permute-start | bytes 614408 | tf_op jit(solution)/shard_map/ppermute | solution.py:21
  21.6 11.4 %collective-permute-start.5 = (bf16[400,256]{1,0:T(8,128)(2,1)S(1)}, bf16[400,256]{1,0:T(8,128)(2,1)S(1)}, u32[]{:S(2)}, u32[]{:S(2)}) collective-permute-start(bf16[400,256]{1,0:T(8,128)(2,1)S(1)} %fusion.3), channel_id=1, source_target_pairs={{0,32},{16,48},{32,0},{48,16},{1,33},{17,49},{33,1},{49,17},{2,34}... | collective-permute-start | bytes 614408 | tf_op jit(solution)/shard_map/ppermute | solution.py:21
  24.6 8.5 %collective-permute-start.6 = (bf16[400,256]{1,0:T(8,128)(2,1)S(1)}, bf16[400,256]{1,0:T(8,128)(2,1)S(1)}, u32[]{:S(2)}, u32[]{:S(2)}) collective-permute-start(bf16[400,256]{1,0:T(8,128)(2,1)S(1)} %fusion.3), channel_id=1, source_target_pairs={{0,48},{16,0},{32,16},{48,32},{1,49},{17,1},{33,17},{49,33},{2,50}... | collective-permute-start | bytes 614408 | tf_op jit(solution)/shard_map/ppermute | solution.py:21
  33.1 14.9 %collective-permute-start.11 = (bf16[4,208,256]{2,1,0:T(8,128)(2,1)S(1)}, bf16[4,208,256]{2,1,0:T(8,128)(2,1)S(1)}, u32[]{:S(2)}, u32[]{:S(2)}) collective-permute-start(bf16[4,208,256]{2,1,0:T(8,128)(2,1)S(1)} %slice.110.refs_0_), channel_id=1, source_target_pairs={{0,1},{1,64},{64,65},{65,0},{2,3},{3,66},{66,67},{67,2},{4,5},{5,6... | collective-permute-start | bytes 1277960 | tf_op jit(solution)/shard_map/ppermute | solution.py:21
  33.8 14.1 %collective-permute-start.12 = (bf16[4,208,256]{2,1,0:T(8,128)(2,1)S(1)}, bf16[4,208,256]{2,1,0:T(8,128)(2,1)S(1)}, u32[]{:S(2)}, u32[]{:S(2)}) collective-permute-start(bf16[4,208,256]{2,1,0:T(8,128)(2,1)S(1)} %slice.110.refs_0_), channel_id=1, source_target_pairs={{0,65},{1,0},{64,1},{65,64},{2,67},{3,2},{66,3},{67,66},{4,69},{5,... | collective-permute-start | bytes 1277960 | tf_op jit(solution)/shard_map/ppermute | solution.py:21
  36.5 10.1 %collective-permute-start.13 = (bf16[4,192,256]{2,1,0:T(8,128)(2,1)S(1)}, bf16[4,192,256]{2,1,0:T(8,128)(2,1)S(1)}, u32[]{:S(2)}, u32[]{:S(2)}) collective-permute-start(bf16[4,192,256]{2,1,0:T(8,128)(2,1)S(1)} %get-tuple-element.71.refs_4_), channel_id=1, source_target_pairs={{0,16},{16,32},{32,48},{48,0},{1,17},{17,33},{33,49},{49,1},{2,18}... | collective-permute-start | bytes 1179656 | tf_op jit(solution)/shard_map/ppermute | solution.py:21
  38.2 9.8 %collective-permute-start.14 = (bf16[4,192,256]{2,1,0:T(8,128)(2,1)S(1)}, bf16[4,192,256]{2,1,0:T(8,128)(2,1)S(1)}, u32[]{:S(2)}, u32[]{:S(2)}) collective-permute-start(bf16[4,192,256]{2,1,0:T(8,128)(2,1)S(1)} %get-tuple-element.71.refs_4_), channel_id=1, source_target_pairs={{0,48},{16,0},{32,16},{48,32},{1,49},{17,1},{33,17},{49,33},{2,50}... | collective-permute-start | bytes 1179656 | tf_op jit(solution)/shard_map/ppermute | solution.py:21
  48.0 0.8 copy-start.2
  48.0 1.0 copy-start.3
  48.8 32.5 %collective-permute-start.19 = (bf16[1002,4096]{1,0:T(8,128)(2,1)}, bf16[1002,4096]{1,0:T(8,128)(2,1)}, u32[]{:S(2)}, u32[]{:S(2)}) collective-permute-start(bf16[1002,4096]{1,0:T(8,128)(2,1)} %bitcast.30.refs_8_), channel_id=1, source_target_pairs={{0,8},{8,0},{1,9},{9,1},{2,10},{10,2},{3,11},{11,3},{4,12},{12,4},... | collective-permute-start | bytes 24625160 | tf_op jit(solution)/shard_map/ppermute | solution.py:25
  49.0 14.3 %collective-permute-start.10 = (bf16[4,208,256]{2,1,0:T(8,128)(2,1)S(1)}, bf16[4,208,256]{2,1,0:T(8,128)(2,1)}, u32[]{:S(2)}, u32[]{:S(2)}) collective-permute-start(bf16[4,208,256]{2,1,0:T(8,128)(2,1)S(1)} %slice.110.refs_0_), channel_id=1, source_target_pairs={{0,64},{1,65},{64,0},{65,1},{2,66},{3,67},{66,2},{67,3},{4,68},{5,... | collective-permute-start | bytes 1277960 | tf_op jit(solution)/shard_map/ppermute | solution.py:21
  49.1 32.2 %copy-start = (s32[4]{0:T(128)}, s32[4]{0:T(128)S(1)}, u32[]{:S(2)}) copy-start(s32[4]{0:T(128)S(1)} %pad_add_fusion.ids_ref) | copy-start | bytes 52
  49.5 2.0 %copy-start.1 = (bf16[4,400,256]{2,0,1:T(4,128)(2,1)}, bf16[4,400,256]{2,0,1:T(4,128)(2,1)S(1)}, u32[]{:S(2)}) copy-start(bf16[4,400,256]{2,0,1:T(4,128)(2,1)S(1)} %copy.23) | copy-start | bytes 2457604
  49.5 16.3 %collective-permute-start.15 = (bf16[4,192,256]{2,1,0:T(8,128)(2,1)S(1)}, bf16[4,192,256]{2,1,0:T(8,128)(2,1)}, u32[]{:S(2)}, u32[]{:S(2)}) collective-permute-start(bf16[4,192,256]{2,1,0:T(8,128)(2,1)S(1)} %get-tuple-element.71.refs_4_), channel_id=1, source_target_pairs={{0,32},{16,48},{32,0},{48,16},{1,33},{17,49},{33,1},{49,17},{2,34}... | collective-permute-start | bytes 1179656 | tf_op jit(solution)/shard_map/ppermute | solution.py:21
  51.5 29.8 %collective-permute-start.16 = (bf16[4,192,256]{2,1,0:T(8,128)(2,1)S(1)}, bf16[4,192,256]{2,1,0:T(8,128)(2,1)S(1)}, u32[]{:S(2)}, u32[]{:S(2)}) collective-permute-start(bf16[4,192,256]{2,1,0:T(8,128)(2,1)S(1)} %slice.116.refs_0_), channel_id=1, source_target_pairs={{0,1},{1,64},{64,65},{65,0},{2,3},{3,66},{66,67},{67,2},{4,5},{5,6... | collective-permute-start | bytes 1179656 | tf_op jit(solution)/shard_map/ppermute | solution.py:21
  52.2 29.0 %collective-permute-start.17 = (bf16[4,192,256]{2,1,0:T(8,128)(2,1)S(1)}, bf16[4,192,256]{2,1,0:T(8,128)(2,1)S(1)}, u32[]{:S(2)}, u32[]{:S(2)}) collective-permute-start(bf16[4,192,256]{2,1,0:T(8,128)(2,1)S(1)} %slice.116.refs_0_), channel_id=1, source_target_pairs={{0,64},{1,65},{64,0},{65,1},{2,66},{3,67},{66,2},{67,3},{4,68},{5,... | collective-permute-start | bytes 1179656 | tf_op jit(solution)/shard_map/ppermute | solution.py:21
  56.0 25.2 %all-to-all-start = ((bf16[4,4,192,256]{3,2,1,0:T(8,128)(2,1)}), bf16[4,4,192,256]{3,2,1,0:T(8,128)(2,1)}, u32[]{:S(2)}, u32[]{:S(2)}) async-start(bf16[4,4,192,256]{3,2,1,0:T(8,128)(2,1)} %broadcast_in_dim.85), calls=%async_computation | async-start | bytes 3145728 | tf_op jit(solution)/shard_map/all_to_all | solution.py:265
  63.3 18.0 %collective-permute-start.18 = (bf16[4,192,256]{2,1,0:T(8,128)(2,1)S(1)}, bf16[4,192,256]{2,1,0:T(8,128)(2,1)S(1)}, u32[]{:S(2)}, u32[]{:S(2)}) collective-permute-start(bf16[4,192,256]{2,1,0:T(8,128)(2,1)S(1)} %slice.116.refs_0_), channel_id=1, source_target_pairs={{0,65},{1,0},{64,1},{65,64},{2,67},{3,2},{66,3},{67,66},{4,69},{5,... | collective-permute-start | bytes 1179656 | tf_op jit(solution)/shard_map/ppermute | solution.py:21
  95.9 22.6 %all-to-all-start.1 = ((f32[64,8,384]{2,1,0:T(8,128)}), f32[64,8,384]{2,1,0:T(8,128)S(1)}, u32[]{:S(2)}, u32[]{:S(2)}) async-start(f32[64,8,384]{2,1,0:T(8,128)} %get-tuple-element.50), calls=%async_computation.1 | async-start | bytes 1572864 | tf_op jit(solution)/shard_map/all_to_all | solution.py:294
  105.0 39.0 %collective-permute-start.21 = (bf16[384,4096]{1,0:T(8,128)(2,1)}, bf16[384,4096]{1,0:T(8,128)(2,1)}, u32[]{:S(2)}, u32[]{:S(2)}) collective-permute-start(bf16[384,4096]{1,0:T(8,128)(2,1)} %get-tuple-element.58.hidden_a), channel_id=1, source_target_pairs={{0,8},{8,0},{1,9},{9,1},{2,10},{10,2},{3,11},{11,3},{4,12},{12,4},... | collective-permute-start | bytes 9437192 | tf_op jit(solution)/shard_map/ppermute | solution.py:25
  135.0 44.4 %all-to-all-start.2 = ((bf16[64,48,512]{2,1,0:T(8,128)(2,1)}), bf16[64,48,512]{2,1,0:T(8,128)(2,1)S(1)}, u32[]{:S(2)}, u32[]{:S(2)}) async-start(bf16[64,48,512]{2,1,0:T(8,128)(2,1)} %bitcast.87), calls=%async_computation.2 | async-start | bytes 6291456 | tf_op jit(solution)/shard_map/all_to_all | solution.py:323
  140.9 3.1 %collective-permute-start.20 = (bf16[1002,384]{1,0:T(8,128)(2,1)}, bf16[1002,384]{1,0:T(8,128)(2,1)}, u32[]{:S(2)}, u32[]{:S(2)}) collective-permute-start(bf16[1002,384]{1,0:T(8,128)(2,1)} %get-tuple-element.57), channel_id=1, source_target_pairs={{0,8},{8,0},{1,9},{9,1},{2,10},{10,2},{3,11},{11,3},{4,12},{12,4},... | collective-permute-start | bytes 2308616 | tf_op jit(solution)/shard_map/ppermute | solution.py:25
  141.8 1.7 collective-permute-start.22
